TPU v7x, 1024 devices: a whole 8x8x8 slice. The times are simulated.
1024 devices in a mesh: table: 16 (over x, core), rep: 64 (over z, y).
Axes of the slice: x: 8, y: 8, z: 8, core: 2. Of those that a mesh axis runs over, the one named last changes fastest.
Arguments:
- tokens: bfloat16 [131072, 512], P(('table', 'rep')), may hold values from -6 to 6
- cotangent: bfloat16 [131072, 512], P(('table', 'rep')), may hold values from -6 to 6
- hist_len: int32 [2048], P(('table', 'rep')), may hold values from 16 to 64, as said below
- item_owner: int32 [131072, 1], P(('table', 'rep')), may hold values from 0 to 15; in each aligned block of 128 rows (0 to 127, 128 to 255, ...) at most 16 rows name the same one
- item_slot: int32 [131072], P(('table', 'rep')), may hold values from 0 to 511
- w_in: bfloat16 [512, 2048], replicated, may hold values from -0.25 to 0.25
- w_out: bfloat16 [512, 512], replicated, may hold values from -0.25 to 0.25
Outputs:
- touched_grad: float32 [8192, 512], P(('table', 'rep'))
- w_in_grad: float32 [512, 2048], P('table', 'rep')
- w_out_grad: float32 [512, 512], P('table', 'rep')
Inputs may be any that keep to these rules, and one draw needn't show every extreme that they name: `hist_len`: histories are ragged; one of length 64 in every draw. `item_owner`: the rows of one device name any one owner at most 16 times; some owner exactly 16 times in some or all devices.
All inputs are finite; a program needn't handle non-finite values.
Results may differ from a plain program's by a relative error of at most 0.023.
Values may be sent and summed in bfloat16 or wider, within the bound.
A program may use at most 32 MiB of HBM per device.

v0:
```python
import math

import jax
import jax.numpy as jnp
from jax import lax
from jax.sharding import PartitionSpec as P

D = 512
HEADS = 4
DH = 128
UNIQ_DEV = 8


def norm_rows(values):
    middle = jnp.mean(values, axis=-1, keepdims=True)
    centered = values - middle
    inverse = lax.rsqrt(jnp.mean(centered * centered, axis=-1, keepdims=True) + 1e-06)
    return (centered * inverse, inverse)


def norm_back(upstream, normed, inverse):
    first = jnp.mean(upstream, axis=-1, keepdims=True)
    second = jnp.mean(upstream * normed, axis=-1, keepdims=True)
    return inverse * (upstream - first - normed * second)


def silu_grad(values):
    sigma = jax.nn.sigmoid(values)
    return sigma * (1.0 + values * (1.0 - sigma))


def layer_back(tokens, cotangent, lengths, w_in, w_out):
    batch, slots, width = tokens.shape
    feats = HEADS * DH
    score_scale = 1.0 / math.sqrt(DH)
    places = jnp.arange(slots, dtype=jnp.int32)
    valid = places[None, :] < lengths[:, None]
    causal = places[:, None] >= places[None, :]
    keep = (causal[None, :, :] & valid[:, None, :])[:, None, :, :]
    normed, inv_tok = norm_rows(tokens.astype(jnp.float32))
    flat_norm = normed.astype(jnp.bfloat16).reshape(-1, width)
    pre = jnp.dot(flat_norm, w_in, preferred_element_type=jnp.float32)
    hidden = jax.nn.silu(pre).astype(jnp.bfloat16).reshape(batch, slots, 4, HEADS, DH)
    gate_u = hidden[:, :, 0]
    vals = hidden[:, :, 1]
    query = hidden[:, :, 2]
    keys = hidden[:, :, 3]
    score = (
        jnp.einsum("bihd,bjhd->bhij", query, keys, preferred_element_type=jnp.float32) * score_scale
    )
    att = jnp.where(keep, jax.nn.silu(score) / slots, 0.0).astype(jnp.bfloat16)
    mixed = jnp.einsum("bhij,bjhd->bihd", att, vals, preferred_element_type=jnp.float32).reshape(
        batch, slots, feats
    )
    on_mix, inv_mix = norm_rows(mixed)
    gate_f = gate_u.reshape(batch, slots, feats).astype(jnp.float32)
    gated = (on_mix * gate_f).astype(jnp.bfloat16)
    err = jnp.where(valid[:, :, None], cotangent, jnp.zeros_like(cotangent))
    flat_err = err.reshape(-1, width)
    part_out = lax.dot_general(
        gated.reshape(-1, feats),
        flat_err,
        (((0,), (0,)), ((), ())),
        preferred_element_type=jnp.float32,
    )
    dgate = lax.dot_general(
        flat_err, w_out, (((1,), (1,)), ((), ())), preferred_element_type=jnp.float32
    ).reshape(batch, slots, feats)
    grad_u = dgate * on_mix
    dmix = norm_back(dgate * gate_f, on_mix, inv_mix).astype(jnp.bfloat16)
    dmix_h = dmix.reshape(batch, slots, HEADS, DH)
    datt = jnp.einsum("bihd,bjhd->bhij", dmix_h, vals, preferred_element_type=jnp.float32)
    dscore = jnp.where(keep, datt * silu_grad(score) / slots, 0.0).astype(jnp.bfloat16)
    grad_v = jnp.einsum("bhij,bihd->bjhd", att, dmix_h, preferred_element_type=jnp.float32)
    grad_q = (
        jnp.einsum("bhij,bjhd->bihd", dscore, keys, preferred_element_type=jnp.float32)
        * score_scale
    )
    grad_k = (
        jnp.einsum("bhij,bihd->bjhd", dscore, query, preferred_element_type=jnp.float32)
        * score_scale
    )
    grad_h = jnp.concatenate(
        [
            grad_u,
            grad_v.reshape(batch, slots, feats),
            grad_q.reshape(batch, slots, feats),
            grad_k.reshape(batch, slots, feats),
        ],
        axis=-1,
    )
    dpre = (grad_h.reshape(-1, 4 * feats) * silu_grad(pre)).astype(jnp.bfloat16)
    part_in = lax.dot_general(
        flat_norm, dpre, (((0,), (0,)), ((), ())), preferred_element_type=jnp.float32
    )
    dnorm = lax.dot_general(
        dpre, w_in, (((1,), (1,)), ((), ())), preferred_element_type=jnp.float32
    ).reshape(batch, slots, width)
    rows = (err.astype(jnp.float32) + norm_back(dnorm, normed, inv_tok)).astype(jnp.bfloat16)
    return (rows.reshape(-1, width), part_in, part_out)


def on_device(tokens, cotangent, hist_len, item_owner, item_slot, w_in, w_out):
    n_table = lax.axis_size("table")
    n_rep = lax.axis_size("rep")
    local_rows = tokens.shape[0]
    rows, part_in, part_out = layer_back(
        tokens.reshape(2, -1, D), cotangent.reshape(2, -1, D), hist_len, w_in, w_out
    )
    owners = item_owner[:, 0]
    capacity = (2 * local_rows // n_table + 7) // 8 * 8
    onehot = (owners[:, None] == jnp.arange(n_table, dtype=jnp.int32)[None, :]).astype(jnp.int32)
    earlier = jnp.cumsum(onehot, axis=0) - onehot
    placed = jnp.sum(earlier * onehot, axis=1)
    outgoing = jnp.zeros((n_table, capacity, D), jnp.bfloat16).at[owners, placed].set(rows)
    out_slots = jnp.zeros((n_table, capacity), jnp.int32).at[owners, placed].set(item_slot)
    incoming, in_slots = (
        lax.all_to_all(outgoing, "table", split_axis=0, concat_axis=0, tiled=True),
        lax.all_to_all(out_slots, "table", split_axis=0, concat_axis=0, tiled=True),
    )
    buffer = (
        jnp.zeros((UNIQ_DEV * n_rep, D), jnp.float32)
        .at[in_slots.reshape(-1)]
        .add(incoming.reshape(-1, D).astype(jnp.float32))
    )
    touched = lax.psum_scatter(buffer, "rep", scatter_dimension=0, tiled=True)
    scale = 1.0 / math.sqrt(local_rows * n_table * n_rep)
    scaled_in = part_in * scale
    scaled_out = part_out * scale
    first_in, first_out = (
        lax.psum_scatter(
            scaled_in.astype(jnp.bfloat16), "table", scatter_dimension=0, tiled=True
        ).astype(jnp.float32),
        lax.psum_scatter(
            scaled_out.astype(jnp.bfloat16), "table", scatter_dimension=0, tiled=True
        ).astype(jnp.float32),
    )
    grad_in, grad_out = (
        lax.psum_scatter(first_in, "rep", scatter_dimension=1, tiled=True),
        lax.psum_scatter(first_out, "rep", scatter_dimension=1, tiled=True),
    )
    return (touched, grad_in, grad_out)


def solution(mesh):
    return jax.shard_map(
        on_device,
        mesh=mesh,
        in_specs=(
            P(("table", "rep"), None),
            P(("table", "rep"), None),
            P(("table", "rep")),
            P(("table", "rep"), None),
            P(("table", "rep")),
            P(),
            P(),
        ),
        out_specs=(P(("table", "rep"), None), P("table", "rep"), P("table", "rep")),
        check_vma=False,
    )
```

profile of v0, /device:TPU:8, one launch (start us, length us, event | category | flops | bytes accessed | tf_op | source)
XLA Modules:
  0.0 458.7 jit_solution(15186040177597269215)
XLA Ops:
  8.0 0.0 copy-start
  8.0 0.0 reduce-scatter.7.cloned.1.call-start
  8.1 1.1 convert_reduce_fusion
  9.2 1.1 fusion.23
  10.4 2.4 multiply_convert_fusion.1
  12.8 0.4 reshape.218
  13.2 0.2 fusion.44
  13.4 0.1 copy-done.19
  13.5 0.1 iota_compare_fusion.2
  13.5 0.6 lt.60
  14.2 0.2 convolution_multiply_fusion.3
  14.4 0.3 bitcast_reduce_fusion
  14.7 0.2 multiply_reduce_fusion.1
  14.9 0.6 add_rsqrt_fusion
  15.5 0.2 copy.45
  15.7 0.1 reshape.221
  15.8 0.7 broadcast_select_fusion
  16.6 1.5 fusion.43
  18.1 0.8 fusion.27
  18.9 0.3 convolution_bitcast_fusion.1
  19.2 0.2 fusion.6
  19.4 0.2 fusion.2
  19.6 0.2 fusion.3
  19.9 0.2 copy.48
  20.1 0.2 copy.50
  20.3 0.2 copy.52
  20.5 0.1 copy-done.2
  20.7 0.4 fusion.7
  21.1 0.2 copy-done.1
  21.2 2.2 multiply_convert_fusion
  23.4 0.0 reduce-scatter.7.cloned.1.call-update
  23.4 0.1 fusion.36
  23.5 0.2 reduce_window_sum.11
  23.7 0.8 select_reduce_fusion
  24.5 0.7 fusion.38
  25.2 0.6 broadcast_in_dim.33
  25.8 18.5 %scatter_fusion = s32[16,16]{1,0:T(8,128)} fusion(s32[16,16]{1,0:T(8,128)} %broadcast_in_dim.33, s32[128]{0:T(128)S(1)} %fusion.38, s32[128]{0:T(128)} %param.11), kind=kCustom, calls=%fused_computation | custom fusion | bytes 2560 | tf_op jit(solution)/shard_map/scatter | solution.py:116
  44.3 16.4 %all-to-all-start = ((s32[16,1,16]{2,1,0:T(1,128)}), s32[16,1,16]{2,1,0:T(1,128)S(1)}, u32[]{:S(2)}, u32[]{:S(2)}) async-start(s32[16,1,16]{2,1,0:T(1,128)} %bitcast.4), calls=%async_computation | async-start | bytes 16384 | tf_op jit(solution)/shard_map/all_to_all | solution.py:119
  60.7 0.0 reduce-scatter.9.cloned.1.call-start
  60.8 1.2 fusion.1
  62.0 0.0 reduce-scatter.9.cloned.1.call-update
  62.0 0.9 fusion.42
  62.9 0.2 fusion.22
  63.1 0.8 broadcast_in_dim.34
  63.9 16.7 %scatter_fusion.1 = bf16[16,16,512]{2,1,0:T(8,128)(2,1)} fusion(bf16[16,16,512]{2,1,0:T(8,128)(2,1)} %broadcast_in_dim.34, s32[128]{0:T(128)S(1)} %fusion.38, bf16[128,512]{1,0:T(8,128)(2,1)S(1)} %fusion.22), kind=kCustom, calls=%fused_computation.1 | custom fusion | bytes 394240 | tf_op jit(solution)/shard_map/scatter | solution.py:115
  80.6 7.2 %all-to-all-start.1 = ((bf16[16,16,512]{2,1,0:T(8,128)(2,1)}), bf16[16,16,512]{2,1,0:T(8,128)(2,1)S(1)}, u32[]{:S(2)}, u32[]{:S(2)}) async-start(bf16[16,16,512]{2,1,0:T(8,128)(2,1)} %scatter_fusion.1), calls=%async_computation.1 | async-start | bytes 524288 | tf_op jit(solution)/shard_map/all_to_all | solution.py:118
  87.8 0.0 all-reduce.5.cloned.1.call-start
  87.9 0.5 broadcast.245
  88.4 0.7 reduce.9
  89.1 0.1 reshape.217
  89.2 6.9 %all-to-all-done.1 = bf16[16,16,512]{2,1,0:T(8,128)(2,1)S(1)} async-done(((bf16[16,16,512]{2,1,0:T(8,128)(2,1)}), bf16[16,16,512]{2,1,0:T(8,128)(2,1)S(1)}, u32[]{:S(2)}, u32[]{:S(2)}) %all-to-all-start.1) | async-done | bytes 262176 | tf_op jit(solution)/shard_map/all_to_all | solution.py:118
  96.1 3.1 scatter_custom_fusion.2
  99.2 0.0 all-reduce.5.cloned.1.call-update
  99.2 0.0 reduce-scatter.11.cloned.1.call-start
  99.3 2.0 reduce-scatter.7.cloned.1.call-done
  101.3 2.1 copy.57
  103.4 0.0 reduce-scatter.11.cloned.1.call-update
  103.4 1.3 dynamic-slice
  105.3 61.1 %reduce-scatter.9.cloned.1.call-done = bf16[32,512]{1,0:T(8,128)(2,1)} async-done(((bf16[512,512]{1,0:T(8,128)(2,1)}), bf16[32,512]{1,0:T(8,128)(2,1)}) %reduce-scatter.9.cloned.1.call-update) | async-done | bytes 32784 | tf_op jit(solution)/shard_map/reduce_scatter | solution.py:134
  166.4 281.7 %all-reduce.6 = f32[32,512]{1,0:T(8,128)S(1)} all-reduce(bf16[32,512]{1,0:T(8,128)(2,1)} %reduce-scatter.9.cloned.1.call-done), channel_id=6, replica_groups=mesh['table'=16,'rep'=64] {'rep'}, use_global_device_ids=true, to_apply=%region_17.18.clone | all-reduce | flops 16384 | bytes 98304
  448.1 0.1 constant_dynamic-slice_fusion
  448.2 0.7 copy.54
  448.9 1.3 constant_dynamic-slice_fusion.1
  450.2 1.4 copy.58
  (52 shorter events, 0.2 us)
Async XLA Ops:
  8.0 2.3 copy-start
  8.0 93.3 %reduce-scatter.7.cloned.1.call-start = ((), (), s32[]{:S(2)}) async-start(), calls=%async_computation.5 | async-start | bytes 2228224 | tf_op jit(solution)/shard_map/reduce_scatter | solution.py:131
  9.2 3.6 copy-start.13
  10.4 2.5 copy-start.15
  12.8 0.7 copy-start.19
  13.5 2.2 copy-start.6
  13.5 2.3 copy-start.3
  14.2 1.3 copy-start.8
  14.4 1.1 copy-start.4
  14.7 0.8 copy-start.10
  15.5 3.5 copy-start.9
  15.8 3.1 copy-start.5
  15.8 3.4 copy-start.7
  19.4 1.2 copy-start.2
  20.2 1.0 copy-start.1
  20.3 1.0 copy-start.14
  20.3 1.0 copy-start.16
  21.2 2.2 copy-start.17
  23.4 37.3 %copy-start.11 = (f32[2,64]{1,0:T(2,128)S(1)}, f32[2,64]{1,0:T(2,128)}, u32[]{:S(2)}) copy-start(f32[2,64]{1,0:T(2,128)} %copy-done.10) | copy-start | bytes 1540
  23.4 37.4 %copy-start.12 = (f32[2,64]{1,0:T(2,128)S(1)}, f32[2,64]{1,0:T(2,128)}, u32[]{:S(2)}) copy-start(f32[2,64]{1,0:T(2,128)} %add_rsqrt_fusion) | copy-start | bytes 1540
  44.3 36.3 %all-to-all-start = ((s32[16,1,16]{2,1,0:T(1,128)}), s32[16,1,16]{2,1,0:T(1,128)S(1)}, u32[]{:S(2)}, u32[]{:S(2)}) async-start(s32[16,1,16]{2,1,0:T(1,128)} %bitcast.4), calls=%async_computation | async-start | bytes 16384 | tf_op jit(solution)/shard_map/all_to_all | solution.py:119
  60.7 2.2 copy-start.18
  60.7 105.7 %reduce-scatter.9.cloned.1.call-start = ((), (), s32[]{:S(2)}) async-start(), calls=%async_computation.6 | async-start | bytes 557056 | tf_op jit(solution)/shard_map/reduce_scatter | solution.py:134
  80.6 15.5 %all-to-all-start.1 = ((bf16[16,16,512]{2,1,0:T(8,128)(2,1)}), bf16[16,16,512]{2,1,0:T(8,128)(2,1)S(1)}, u32[]{:S(2)}, u32[]{:S(2)}) async-start(bf16[16,16,512]{2,1,0:T(8,128)(2,1)} %scatter_fusion.1), calls=%async_computation.1 | async-start | bytes 524288 | tf_op jit(solution)/shard_map/all_to_all | solution.py:118
  87.8 361.1 %all-reduce.5.cloned.1.call-start = ((), (), s32[]{:S(2)}) async-start(), calls=%async_computation.8 | async-start | bytes 2097152
  99.2 351.0 %reduce-scatter.11.cloned.1.call-start = ((), (), s32[]{:S(2)}) async-start(), calls=%async_computation.7 | async-start | bytes 1064960
Sparse Core Ops, SparseCore 0:
  23.6 77.6 reduce-scatter.6
  105.0 61.3 reduce-scatter.8
  171.6 254.0 reduce-scatter.10
Sparse Core Ops, SparseCore 1:
  99.3 176.1 all-reduce.4
where the time goes:
time: 460 us; the launch traced here: 459 us
  blocking collectives  282 us (61%)
  waiting for transfers between devices  70.1 us (15%)
  local copies, waits for them, and re-layouts  46.5 us (10%)
  starting transfers between devices  23.8 us (5%)
  between operations  16.3 us (4%)
  other arithmetic  10.8 us (2%)
  matrix products  9.56 us (2%)
    unnamed x1, blocking collectives  282 us
    reduce_scatter x1, waiting for transfers between devices, on_device(): lax.psum_scatter(scaled_out.astype(jnp.bfloat16), 'table', scatter_dimens...  61.1 us
    scatter x1, local copies, waits for them, and re-layouts, on_device(): jnp.zeros((n_table, capacity), jnp.int32).at[owners, placed].set(item_slot)  18.5 us
    scatter x1, local copies, waits for them, and re-layouts, on_device(): jnp.zeros((n_table, capacity, D), jnp.bfloat16).at[owners, placed].set(rows)  16.7 us
    all_to_all x1, starting transfers between devices, on_device(): lax.all_to_all(out_slots, 'table', split_axis=0, concat_axis=0, tiled=True)  16.4 us
  transfers between devices with their start and end apart: 6, of which 3 were waited for; matrix products, arithmetic and copies ran while one was open for 11% of the time, Pallas kernels for 0%

commit v1 on v0

v1 whole, which is shorter than its diff:
```python
import math

import jax
import jax.numpy as jnp
from jax import lax
from jax.experimental import pallas as pl
from jax.experimental.pallas import tpu as pltpu
from jax.sharding import PartitionSpec as P

D = 512
HEADS = 4
DH = 128
SLOTS_H = 64
TOK = 128
F32 = jnp.float32
BF16 = jnp.bfloat16
MESH = pl.DeviceIdType.MESH
NT = (((1,), (1,)), ((), ()))
TN = (((0,), (0,)), ((), ()))


def mm(a, b, dims=(((1,), (0,)), ((), ()))):
    return lax.dot_general(a, b, dims, preferred_element_type=F32)


def norm_rows(values):
    middle = jnp.mean(values, axis=-1, keepdims=True)
    centered = values - middle
    inverse = lax.rsqrt(jnp.mean(centered * centered, axis=-1, keepdims=True) + 1e-06)
    return centered * inverse, inverse


def norm_back(upstream, normed, inverse):
    first = jnp.mean(upstream, axis=-1, keepdims=True)
    second = jnp.mean(upstream * normed, axis=-1, keepdims=True)
    return inverse * (upstream - first - normed * second)


def sigmoid(values):
    return 0.5 * jnp.tanh(0.5 * values) + 0.5


def iota(shape, dim):
    return lax.broadcasted_iota(jnp.int32, shape, dim)


def cells(block):
    lo = block[:, :128].reshape(64, 8, 128)
    hi = block[:, 128:].reshape(64, 8, 128)
    return jnp.concatenate([lo, hi], axis=1).reshape(8, 8, 16, 128).astype(BF16)


def kernel(
    len_ref, tok_ref, cot_ref, own_ref, slot_ref, w_in_hbm, w_out_hbm,
    touched_ref, gin_ref, gout_ref,
    w_in, w_out, sgrad, hid, d2, nb2, gt2, er2, nbf, gtf,
    out_rows, in_rows, a_own, a_recv, b_own, b_recv,
    t1_own, t1_recv, t2_own, t2_recv,
    a2_own, a2_recv, b2_own, b2_recv, t3_own, t3_recv, t4_own, t4_recv,
    x_own, x_recv, flip,
    w_sem, pair_s, pair_r, row_s, row_r, a_s, a_r, b_s, b_r,
    t1_s, t1_r, t2_s, t2_r, a2_s, a2_r, b2_s, b2_r, t3_s, t3_r, t4_s, t4_r, x_s, x_r,
):
    t = lax.axis_index("table")
    r = lax.axis_index("rep")
    x, core = lax.div(t, 2), lax.rem(t, 2)
    z, y = lax.div(r, 8), lax.rem(r, 8)

    def turn(base, k, n=8):
        return lax.rem(base + (k + n), n)

    def at_z(k):
        return (t, turn(z, k) * 8 + y)

    def at_y(k):
        return (t, z * 8 + turn(y, k))

    def at_t(k):
        return (turn(t, k, 16), r)

    def at_x(k):
        return (turn(x, k) * 2 + core, r)

    mate = (x * 2 + (1 - core), r)
    sent = []

    def push(src, dst, ssem, rsem, where):
        copy = pltpu.make_async_remote_copy(
            src_ref=src, dst_ref=dst, send_sem=ssem, recv_sem=rsem,
            device_id=where, device_id_type=MESH,
        )
        copy.start()
        sent.append(copy)
        return copy

    barrier = pltpu.get_barrier_semaphore()
    partners = [at_z(k) for k in range(1, 8)] + [at_y(k) for k in range(1, 8)]
    partners += [at_t(k) for k in range(1, 16)]
    for where in partners:
        pl.semaphore_signal(barrier, inc=1, device_id=where, device_id_type=MESH)

    loads = []
    for b in range(4):
        cols = pl.ds(b * 512, 512)
        loads.append(pltpu.make_async_copy(w_in_hbm.at[:, cols], w_in.at[:, cols], w_sem.at[b]))
    loads.append(pltpu.make_async_copy(w_out_hbm, w_out, w_sem.at[4]))
    for load in loads:
        load.start()

    len0, len1 = len_ref[0], len_ref[1]
    ri, ci = iota((TOK, TOK), 0), iota((TOK, TOK), 1)
    same = (ri < SLOTS_H) == (ci < SLOTS_H)
    limit = jnp.where(ci < SLOTS_H, len0, len1 + SLOTS_H)
    keep = same & (ci <= ri) & (ci < limit)
    rows_i = iota((TOK, D), 0)
    valid = rows_i < jnp.where(rows_i < SLOTS_H, len0, len1 + SLOTS_H)

    normed, inv_tok = norm_rows(tok_ref[...].astype(F32))
    nb = normed.astype(BF16)
    pi, pj = iota((D, D), 0), iota((D, D), 1)
    source = ((pj // 32) % 8) * 64 + (pj // 256) * 32 + pj % 32
    perm = jnp.where(pi == source, 1.0, 0.0).astype(BF16)
    nbp = mm(nb, perm).astype(BF16)
    nbf[0] = nbp[:, :256]
    nbf[1] = nbp[:, 256:]
    nb2[0:TOK, :] = nbf[core]
    err = jnp.where(valid, cot_ref[...], jnp.zeros((TOK, D), BF16))
    er2[0:TOK, :] = err
    for b in range(4):
        cols = pl.ds(b * 512, 512)
        loads[b].wait()
        pre = mm(nb, w_in[:, cols])
        sig = sigmoid(pre)
        hid[:, cols] = (pre * sig).astype(BF16)
        sgrad[:, cols] = sig * (1.0 + pre * (1.0 - sig))
    pl.semaphore_wait(barrier, len(partners))
    pair = [
        push(er2.at[pl.ds(0, TOK)], er2.at[pl.ds(TOK, TOK)], pair_s.at[0], pair_r.at[0], mate),
        push(nbf.at[1 - core], nb2.at[pl.ds(TOK, TOK)], pair_s.at[1], pair_r.at[1], mate),
    ]
    score_scale = 1.0 / math.sqrt(DH)
    atts, slopes, mixes = [], [], []
    for h in range(HEADS):
        query = hid[:, 1024 + h * DH:1024 + (h + 1) * DH]
        keys = hid[:, 1536 + h * DH:1536 + (h + 1) * DH]
        vals = hid[:, 512 + h * DH:512 + (h + 1) * DH]
        score = mm(query, keys, NT) * score_scale
        sig = sigmoid(score)
        att = jnp.where(keep, score * sig * (1.0 / SLOTS_H), 0.0).astype(BF16)
        slopes.append(jnp.where(keep, sig * (1.0 + score * (1.0 - sig)) * (1.0 / SLOTS_H), 0.0))
        atts.append(att)
        mixes.append(mm(att, vals))
    on_mix, inv_mix = norm_rows(jnp.concatenate(mixes, axis=1))
    gate = hid[:, 0:512].astype(F32)
    gated = (on_mix * gate).astype(BF16)
    gtp = mm(gated, perm).astype(BF16)
    gtf[0] = gtp[:, :256]
    gtf[1] = gtp[:, 256:]
    gt2[0:TOK, :] = gtf[core]
    pair.append(push(gtf.at[1 - core], gt2.at[pl.ds(TOK, TOK)], pair_s.at[2], pair_r.at[2], mate))

    loads[4].wait()
    dgate = mm(err, w_out[...], NT)

    def give(b, value):
        cols = pl.ds(b * 512, 512)
        d2[0:TOK, cols] = (value * sgrad[:, cols]).astype(BF16)
        pair.append(push(
            d2.at[pl.ds(0, TOK), cols], d2.at[pl.ds(TOK, TOK), cols],
            pair_s.at[3 + b], pair_r.at[3 + b], mate,
        ))

    give(0, dgate * on_mix)
    dmix = norm_back(dgate * gate, on_mix, inv_mix).astype(BF16)
    gv, gq, gk = [], [], []
    for h in range(HEADS):
        query = hid[:, 1024 + h * DH:1024 + (h + 1) * DH]
        keys = hid[:, 1536 + h * DH:1536 + (h + 1) * DH]
        vals = hid[:, 512 + h * DH:512 + (h + 1) * DH]
        part = dmix[:, h * DH:(h + 1) * DH]
        dscore = (mm(part, vals, NT) * slopes[h]).astype(BF16)
        gv.append(mm(atts[h], part, TN))
        gq.append(mm(dscore, keys) * score_scale)
        gk.append(mm(dscore, query, TN) * score_scale)
    give(1, jnp.concatenate(gv, axis=1))
    give(2, jnp.concatenate(gq, axis=1))
    give(3, jnp.concatenate(gk, axis=1))
    dnorm = mm(d2[0:TOK, 0:512], w_in[:, 0:512], NT)
    for b in range(1, 4):
        dnorm += mm(d2[0:TOK, b * 512:(b + 1) * 512], w_in[:, b * 512:(b + 1) * 512], NT)
    rows = (err.astype(F32) + norm_back(dnorm, normed, inv_tok)).astype(BF16)

    owner = own_ref[...]
    slot = slot_ref[...]
    mine = iota((16, TOK), 0) == owner
    hot = jnp.where(mine, 1.0, 0.0)
    before = jnp.where(ri < ci, 1.0, 0.0).astype(BF16)
    earlier = mm(hot.astype(BF16), before)
    placed = jnp.sum(earlier * hot, axis=0, keepdims=True)
    key = owner.astype(F32) * 16.0 + placed
    pick = jnp.where(iota((256, TOK), 0).astype(F32) == key, 1.0, 0.0)
    packed = mm(pick.astype(BF16), rows).astype(BF16)
    s_z = jnp.sum(pick * (slot // 64).astype(F32), axis=1, keepdims=True)
    s_y = jnp.sum(pick * ((slot // 8) % 8).astype(F32), axis=1, keepdims=True)
    s_i = jnp.sum(pick * (slot % 8).astype(F32), axis=1, keepdims=True)
    lane = iota((256, 128), 1)
    tail = jnp.where(lane == 0, s_z, jnp.where(lane == 1, s_y, jnp.where(lane == 2, s_i, 0.0)))
    out_rows[:, :, 0:512] = packed.reshape(16, 16, 512)
    out_rows[:, :, 512:640] = tail.astype(BF16).reshape(16, 16, 128)
    in_rows[0] = out_rows[t]
    row_copies = []
    for k in (8, 7, 9, 6, 10, 5, 11, 4, 12, 3, 13, 2, 14, 1, 15):
        row_copies.append(push(
            out_rows.at[turn(t, k, 16)], in_rows.at[k], row_s.at[k], row_r.at[k], at_t(k)
        ))

    for copy in pair[:3]:
        copy.wait_recv()
    a_own[:, :, 32:48, :] = cells(mm(er2[...], gt2[...], TN))
    for copy in pair[3:]:
        copy.wait_recv()

    def block(k):
        d = turn(z, k)
        cols = pl.ds(pl.multiple_of(d * 256, 256), 256)
        part = mm(d2[:, cols], nb2[...], TN)
        a_own[d, :, 0:32, :] = part[:, :128].reshape(8, 32, 128).astype(BF16)
        b_own[:, d] = part[:, 128:].reshape(8, 32, 128).astype(BF16)

    def ring_step(own, recv, ssem, rsem, base, where, step, previous):
        made = []
        for up in (True, False):
            if not up and step == 3:
                continue
            k = 4 - step if up else step - 3
            slot_no = step if up else 4 + step
            d = turn(base, k)
            if step > 0:
                previous[0 if up else 1].wait_recv()
                own[d] = (own[d].astype(F32) + recv[slot_no - 1].astype(F32)).astype(BF16)
            made.append(push(
                own.at[d], recv.at[slot_no], ssem.at[slot_no], rsem.at[slot_no], where(1 if up else -1)
            ))
        return made if len(made) == 2 else [made[0], previous[1]]

    def ring_end(own, recv, base, previous):
        previous[0].wait_recv()
        previous[1].wait_recv()
        return own[base].astype(F32) + recv[3].astype(F32) + recv[6].astype(F32)

    block(4)
    block(-3)
    ca = ring_step(a_own, a_recv, a_s, a_r, z, at_z, 0, None)
    for k in (3, -2, 2, -1, 1, 0):
        block(k)
    cb = ring_step(b_own, b_recv, b_s, b_r, y, at_y, 0, None)
    ca = ring_step(a_own, a_recv, a_s, a_r, z, at_z, 1, ca)
    cb = ring_step(b_own, b_recv, b_s, b_r, y, at_y, 1, cb)

    for copy in row_copies:
        copy.wait_recv()
    arrived = in_rows[...].reshape(256, 640)
    numbers = arrived[:, 512:640].astype(F32)
    by_z = jnp.where(lane == 0, 64.0, jnp.where(lane == 1, 8.0, jnp.where(lane == 2, 1.0, 0.0)))
    by_y = jnp.where(lane == 0, 8.0, jnp.where(lane == 1, 64.0, jnp.where(lane == 2, 1.0, 0.0)))
    line = iota((256, 512), 1).astype(F32)
    hot_z = jnp.where(line == jnp.sum(numbers * by_z, axis=1, keepdims=True), 1.0, 0.0)
    hot_y = jnp.where(line == jnp.sum(numbers * by_y, axis=1, keepdims=True), 1.0, 0.0)
    t1_own[...] = cells(mm(hot_z.astype(BF16), arrived[:, 0:256], TN))
    t2_own[...] = cells(mm(hot_y.astype(BF16), arrived[:, 256:512], TN))
    ct = []
    for k in (4, 3, 5, 2, 6, 1, 7):
        ct.append(push(t1_own.at[turn(z, k)], t1_recv.at[k], t1_s.at[k], t1_r.at[k], at_z(k)))
        ct.append(push(t2_own.at[turn(y, k)], t2_recv.at[k], t2_s.at[k], t2_r.at[k], at_y(k)))

    for step in (2, 3):
        ca = ring_step(a_own, a_recv, a_s, a_r, z, at_z, step, ca)
        cb = ring_step(b_own, b_recv, b_s, b_r, y, at_y, step, cb)
    a2_own[...] = ring_end(a_own, a_recv, z, ca).astype(BF16)
    c2 = []
    for k in (4, 3, 5, 2, 6, 1, 7):
        c2.append(push(a2_own.at[turn(y, k)], a2_recv.at[k], a2_s.at[k], a2_r.at[k], at_y(k)))
    b2_own[...] = ring_end(b_own, b_recv, y, cb).astype(BF16)
    for k in (4, 3, 5, 2, 6, 1, 7):
        c2.append(push(b2_own.at[turn(z, k)], b2_recv.at[k], b2_s.at[k], b2_r.at[k], at_z(k)))

    for copy in ct:
        copy.wait_recv()

    def total(own, recv, base):
        acc = own[base].astype(F32)
        for k in range(1, 8):
            acc += recv[k].astype(F32)
        return acc

    t3_own[...] = total(t1_own, t1_recv, z).astype(BF16)
    t4_own[...] = total(t2_own, t2_recv, y).astype(BF16)
    c3 = []
    for k in (4, 3, 5, 2, 6, 1, 7):
        c3.append(push(t3_own.at[turn(y, k)], t3_recv.at[k], t3_s.at[k], t3_r.at[k], at_y(k)))
        c3.append(push(t4_own.at[turn(z, k)], t4_recv.at[k], t4_s.at[k], t4_r.at[k], at_z(k)))

    for copy in c2:
        copy.wait_recv()
    a_cell = total(a2_own, a2_recv, y)
    b_cell = total(b2_own, b2_recv, z)
    quarter = iota((8, 128), 1) // 32
    for xh, source_cell in ((0, a_cell), (1, b_cell)):
        for xl in range(4):
            acc = jnp.zeros((8, 128), F32)
            for g in range(4):
                piece = source_cell[8 * g:8 * g + 8]
                if g != xl:
                    piece = pltpu.roll(piece, 32 * ((g - xl) % 4), 1)
                acc = jnp.where(quarter == g, piece, acc)
            both = jnp.concatenate([acc, a_cell[32 + 8 * xh:40 + 8 * xh]], axis=0)
            x_own[xh * 4 + xl] = both.astype(BF16)
    cx = []
    for k in (4, 3, 5, 2, 6, 1, 7):
        cx.append(push(x_own.at[turn(x, k)], x_recv.at[k], x_s.at[k], x_r.at[k], at_x(k)))

    for copy in c3:
        copy.wait_recv()
    left = total(t3_own, t3_recv, y)
    right = total(t4_own, t4_recv, z)
    touched_ref[:, 0:128] = left[0:8]
    touched_ref[:, 128:256] = left[8:16]
    touched_ref[:, 256:384] = right[0:8]
    touched_ref[:, 384:512] = right[8:16]

    for copy in cx:
        copy.wait_recv()
    scale = 1.0 / math.sqrt(TOK * 16 * 64)
    last = total(x_own, x_recv, x) * scale
    turned = jnp.transpose(jnp.concatenate([last, jnp.zeros((112, 128), F32)], axis=0))
    flip[...] = turned
    for g in range(4):
        gin_ref[:, 8 * g:8 * g + 8] = turned[32 * g:32 * g + 32, 0:8]
    gout_ref[...] = flip[pl.ds(pl.multiple_of(lax.rem(x, 4) * 32, 32), 32), :][:, 8:16]

    for copy in sent:
        copy.wait_send()


def on_device(tokens, cotangent, hist_len, item_owner, item_slot, w_in, w_out):
    vmem = pl.BlockSpec(memory_space=pltpu.VMEM)
    hbm = pl.BlockSpec(memory_space=pl.ANY)

    def buf(*shape, dtype=BF16):
        return pltpu.VMEM(shape, dtype)

    def sems(n):
        return pltpu.SemaphoreType.DMA((n,))

    return pl.pallas_call(
        kernel,
        out_shape=(
            jax.ShapeDtypeStruct((8, 512), F32),
            jax.ShapeDtypeStruct((32, 32), F32),
            jax.ShapeDtypeStruct((32, 8), F32),
        ),
        in_specs=[pl.BlockSpec(memory_space=pltpu.SMEM), vmem, vmem, vmem, vmem, hbm, hbm],
        out_specs=(vmem, vmem, vmem),
        scratch_shapes=[
            buf(512, 2048), buf(512, 512), buf(TOK, 2048, dtype=F32), buf(TOK, 2048),
            buf(256, 2048), buf(256, 256), buf(256, 256), buf(256, 512),
            buf(2, TOK, 256), buf(2, TOK, 256),
            buf(16, 16, 640), buf(16, 16, 640),
            buf(8, 8, 48, 128), buf(7, 8, 48, 128), buf(8, 8, 32, 128), buf(7, 8, 32, 128),
            buf(8, 8, 16, 128), buf(8, 8, 16, 128), buf(8, 8, 16, 128), buf(8, 8, 16, 128),
            buf(8, 48, 128), buf(8, 48, 128), buf(8, 32, 128), buf(8, 32, 128),
            buf(8, 16, 128), buf(8, 16, 128), buf(8, 16, 128), buf(8, 16, 128),
            buf(8, 16, 128), buf(8, 16, 128), buf(128, 128, dtype=F32),
            sems(5), sems(7), sems(7), sems(16), sems(16),
            sems(7), sems(7), sems(7), sems(7),
        ] + [sems(8)] * 14,
        compiler_params=pltpu.CompilerParams(
            collective_id=0, has_side_effects=True, vmem_limit_bytes=40 * 1024 * 1024
        ),
    )(
        hist_len, tokens, cotangent, item_owner.reshape(1, TOK), item_slot.reshape(1, TOK),
        w_in, w_out,
    )


def solution(mesh):
    return jax.shard_map(
        on_device,
        mesh=mesh,
        in_specs=(
            P(("table", "rep"), None),
            P(("table", "rep"), None),
            P(("table", "rep")),
            P(("table", "rep"), None),
            P(("table", "rep")),
            P(),
            P(),
        ),
        out_specs=(P(("table", "rep"), None), P("table", "rep"), P("table", "rep")),
        check_vma=False,
    )
```

time: 460 us -> 69.6 us (0.15)
  the two profiles are of different devices: /device:TPU:8 before, /device:TPU:1 now
where the time goes in v1:
time: 69.6 us; the launch traced here: 68.7 us
  Pallas kernels  59.8 us (86%)
  local copies, waits for them, and re-layouts  8.27 us (12%)
    pallas_call x1, Pallas kernels, on_device(): pl.pallas_call(kernel, out_shape=(jax.ShapeDtypeStruct((8, 512), F32), ja...  59.8 us
    unnamed x16, local copies, waits for them, and re-layouts  7.61 us

profile of v1, /device:TPU:1, one launch (start us, length us, event | category | flops | bytes accessed | tf_op | source)
XLA Modules:
  0.0 68.7 jit_solution(11346672722148474249)
XLA Ops:
  0.6 0.0 copy-start
  0.6 1.6 %copy-done = bf16[512,2048]{1,0:T(8,128)(2,1)S(1)} copy-done((bf16[512,2048]{1,0:T(8,128)(2,1)S(1)}, bf16[512,2048]{1,0:T(8,128)(2,1)}, u32[]{:S(2)}) %copy-start) | copy-done | bytes 2097176
  2.2 0.0 copy-start.1
  2.2 1.0 %copy-done.1 = bf16[512,512]{1,0:T(8,128)(2,1)S(1)} copy-done((bf16[512,512]{1,0:T(8,128)(2,1)S(1)}, bf16[512,512]{1,0:T(8,128)(2,1)}, u32[]{:S(2)}) %copy-start.1) | copy-done | bytes 524312
  3.3 0.0 copy-start.2
  3.3 0.9 %copy-done.2 = bf16[128,512]{1,0:T(8,128)(2,1)S(1)} copy-done((bf16[128,512]{1,0:T(8,128)(2,1)S(1)}, bf16[128,512]{1,0:T(8,128)(2,1)}, u32[]{:S(2)}) %copy-start.2) | copy-done | bytes 131096
  4.2 0.0 copy-start.3
  4.2 0.9 %copy-done.3 = bf16[128,512]{1,0:T(8,128)(2,1)S(1)} copy-done((bf16[128,512]{1,0:T(8,128)(2,1)S(1)}, bf16[128,512]{1,0:T(8,128)(2,1)}, u32[]{:S(2)}) %copy-start.3) | copy-done | bytes 131096
  5.1 0.0 copy-start.4
  5.1 0.7 copy-done.4
  5.7 0.0 copy-start.5
  5.7 0.7 copy-done.5
  6.4 0.0 copy-start.6
  6.4 0.7 copy-done.6
  7.0 59.8 %shard_map.94 = (f32[8,512]{1,0:T(8,128)S(1)}, f32[32,32]{1,0:T(8,128)S(1)}, f32[32,8]{1,0:T(8,128)S(1)}) custom-call(s32[2]{0:T(128)S(1)} %copy-done.4, bf16[128,512]{1,0:T(8,128)(2,1)S(1)} %copy-done.2, bf16[128,512]{1,0:T(8,128)(2,1)S(1)} %copy-done.3, s32[1,128]{1,0:T(1,128)S(1)} %bitcast.2, s32[1,128]{1,0:T(1,128)S(1)} %bitcast.3, ...), custom_call_target="tpu_custom_call" | custom-call | tf_op jit(solution)/shard_map/pallas_call | solution.py:355
  66.8 0.7 copy.10
  67.5 0.6 copy.13
  68.1 0.6 copy.14
Async XLA Ops:
  0.6 1.6 %copy-start = (bf16[512,2048]{1,0:T(8,128)(2,1)S(1)}, bf16[512,2048]{1,0:T(8,128)(2,1)}, u32[]{:S(2)}) copy-start(bf16[512,2048]{1,0:T(8,128)(2,1)} %w_in_hbm.1) | copy-start | bytes 6291460
  2.2 1.0 %copy-start.1 = (bf16[512,512]{1,0:T(8,128)(2,1)S(1)}, bf16[512,512]{1,0:T(8,128)(2,1)}, u32[]{:S(2)}) copy-start(bf16[512,512]{1,0:T(8,128)(2,1)} %w_out_hbm.1) | copy-start | bytes 1572868
  3.3 0.9 %copy-start.2 = (bf16[128,512]{1,0:T(8,128)(2,1)S(1)}, bf16[128,512]{1,0:T(8,128)(2,1)}, u32[]{:S(2)}) copy-start(bf16[128,512]{1,0:T(8,128)(2,1)} %tok_ref.1) | copy-start | bytes 393220
  4.2 0.9 %copy-start.3 = (bf16[128,512]{1,0:T(8,128)(2,1)S(1)}, bf16[128,512]{1,0:T(8,128)(2,1)}, u32[]{:S(2)}) copy-start(bf16[128,512]{1,0:T(8,128)(2,1)} %cot_ref.1) | copy-start | bytes 393220
  5.1 0.7 copy-start.4
  5.7 0.7 copy-start.5
  6.4 0.7 copy-start.6

commit v2 on v1

--- a/solution.py
+++ b/solution.py
@@ -51,15 +51,16 @@
 
 
 def kernel(
-    len_ref, tok_ref, cot_ref, own_ref, slot_ref, w_in_hbm, w_out_hbm,
-    touched_ref, gin_ref, gout_ref,
-    w_in, w_out, sgrad, hid, d2, nb2, gt2, er2, nbf, gtf,
+    len_hbm, tok_hbm, cot_hbm, own_hbm, slot_hbm, w_in_hbm, w_out_hbm,
+    touched_ref, last_ref,
+    len_ref, tok_ref, cot_ref, own_ref, slot_ref, w_in, w_out, sgrad, hid, d2, nb2, gt2, er2, nbf, gtf,
     out_rows, in_rows, a_own, a_recv, b_own, b_recv,
     t1_own, t1_recv, t2_own, t2_recv,
     a2_own, a2_recv, b2_own, b2_recv, t3_own, t3_recv, t4_own, t4_recv,
-    x_own, x_recv, flip,
+    x_own, x_recv, o1_own, o1_recv, o2_own, o2_recv, o3_own, o3_recv, flip,
     w_sem, pair_s, pair_r, row_s, row_r, a_s, a_r, b_s, b_r,
     t1_s, t1_r, t2_s, t2_r, a2_s, a2_r, b2_s, b2_r, t3_s, t3_r, t4_s, t4_r, x_s, x_r,
+    o1_s, o1_r, o2_s, o2_r, o3_s, o3_r,
 ):
     t = lax.axis_index("table")
     r = lax.axis_index("rep")
@@ -99,6 +100,12 @@
     for where in partners:
         pl.semaphore_signal(barrier, inc=1, device_id=where, device_id_type=MESH)
 
+    small = []
+    for n, (there, here) in enumerate((
+        (tok_hbm, tok_ref), (len_hbm, len_ref), (cot_hbm, cot_ref), (own_hbm, own_ref), (slot_hbm, slot_ref),
+    )):
+        small.append(pltpu.make_async_copy(there, here, w_sem.at[5 + n]))
+        small[-1].start()
     loads = []
     for b in range(4):
         cols = pl.ds(b * 512, 512)
@@ -107,6 +114,7 @@
     for load in loads:
         load.start()
 
+    small[1].wait()
     len0, len1 = len_ref[0], len_ref[1]
     ri, ci = iota((TOK, TOK), 0), iota((TOK, TOK), 1)
     same = (ri < SLOTS_H) == (ci < SLOTS_H)
@@ -115,6 +123,7 @@
     rows_i = iota((TOK, D), 0)
     valid = rows_i < jnp.where(rows_i < SLOTS_H, len0, len1 + SLOTS_H)
 
+    small[0].wait()
     normed, inv_tok = norm_rows(tok_ref[...].astype(F32))
     nb = normed.astype(BF16)
     pi, pj = iota((D, D), 0), iota((D, D), 1)
@@ -124,6 +133,7 @@
     nbf[0] = nbp[:, :256]
     nbf[1] = nbp[:, 256:]
     nb2[0:TOK, :] = nbf[core]
+    small[2].wait()
     err = jnp.where(valid, cot_ref[...], jnp.zeros((TOK, D), BF16))
     er2[0:TOK, :] = err
     for b in range(4):
@@ -190,6 +200,8 @@
         dnorm += mm(d2[0:TOK, b * 512:(b + 1) * 512], w_in[:, b * 512:(b + 1) * 512], NT)
     rows = (err.astype(F32) + norm_back(dnorm, normed, inv_tok)).astype(BF16)
 
+    small[3].wait()
+    small[4].wait()
     owner = own_ref[...]
     slot = slot_ref[...]
     mine = iota((16, TOK), 0) == owner
@@ -216,7 +228,9 @@
 
     for copy in pair[:3]:
         copy.wait_recv()
-    a_own[:, :, 32:48, :] = cells(mm(er2[...], gt2[...], TN))
+    o1_own[...] = mm(gt2[...], er2[...], TN).astype(BF16).reshape(8, 32, 512)
+    far = (4, 3, 5, 2, 6, 1, 7)
+    co1 = [push(o1_own.at[turn(x, k)], o1_recv.at[k], o1_s.at[k], o1_r.at[k], at_x(k)) for k in far]
     for copy in pair[3:]:
         copy.wait_recv()
 
@@ -224,38 +238,25 @@
         d = turn(z, k)
         cols = pl.ds(pl.multiple_of(d * 256, 256), 256)
         part = mm(d2[:, cols], nb2[...], TN)
-        a_own[d, :, 0:32, :] = part[:, :128].reshape(8, 32, 128).astype(BF16)
+        a_own[d] = part[:, :128].reshape(8, 32, 128).astype(BF16)
         b_own[:, d] = part[:, 128:].reshape(8, 32, 128).astype(BF16)
 
-    def ring_step(own, recv, ssem, rsem, base, where, step, previous):
-        made = []
-        for up in (True, False):
-            if not up and step == 3:
-                continue
-            k = 4 - step if up else step - 3
-            slot_no = step if up else 4 + step
-            d = turn(base, k)
-            if step > 0:
-                previous[0 if up else 1].wait_recv()
-                own[d] = (own[d].astype(F32) + recv[slot_no - 1].astype(F32)).astype(BF16)
-            made.append(push(
-                own.at[d], recv.at[slot_no], ssem.at[slot_no], rsem.at[slot_no], where(1 if up else -1)
-            ))
-        return made if len(made) == 2 else [made[0], previous[1]]
-
-    def ring_end(own, recv, base, previous):
-        previous[0].wait_recv()
-        previous[1].wait_recv()
-        return own[base].astype(F32) + recv[3].astype(F32) + recv[6].astype(F32)
-
-    block(4)
-    block(-3)
-    ca = ring_step(a_own, a_recv, a_s, a_r, z, at_z, 0, None)
-    for k in (3, -2, 2, -1, 1, 0):
+    def spread(own, recv, ssem, rsem, base, where, k):
+        return push(own.at[turn(base, k)], recv.at[k], ssem.at[k], rsem.at[k], where(k))
+
+    ca, cb = [], []
+    for k in far:
         block(k)
-    cb = ring_step(b_own, b_recv, b_s, b_r, y, at_y, 0, None)
-    ca = ring_step(a_own, a_recv, a_s, a_r, z, at_z, 1, ca)
-    cb = ring_step(b_own, b_recv, b_s, b_r, y, at_y, 1, cb)
+        ca.append(spread(a_own, a_recv, a_s, a_r, z, at_z, k))
+    block(0)
+    for k in far:
+        cb.append(spread(b_own, b_recv, b_s, b_r, y, at_y, k))
+
+    def total(own, recv, base):
+        acc = own[base].astype(F32)
+        for k in range(1, 8):
+            acc += recv[k].astype(F32)
+        return acc
 
     for copy in row_copies:
         copy.wait_recv()
@@ -273,25 +274,26 @@
         ct.append(push(t1_own.at[turn(z, k)], t1_recv.at[k], t1_s.at[k], t1_r.at[k], at_z(k)))
         ct.append(push(t2_own.at[turn(y, k)], t2_recv.at[k], t2_s.at[k], t2_r.at[k], at_y(k)))
 
-    for step in (2, 3):
-        ca = ring_step(a_own, a_recv, a_s, a_r, z, at_z, step, ca)
-        cb = ring_step(b_own, b_recv, b_s, b_r, y, at_y, step, cb)
-    a2_own[...] = ring_end(a_own, a_recv, z, ca).astype(BF16)
+    for copy in co1:
+        copy.wait_recv()
+    tall = jnp.transpose(total(o1_own, o1_recv, x)).reshape(8, 4, 16, 32)
+    o2_own[...] = jnp.concatenate([tall[:, g] for g in range(4)], axis=-1).astype(BF16)
+    co2 = [push(o2_own.at[turn(z, k)], o2_recv.at[k], o2_s.at[k], o2_r.at[k], at_z(k)) for k in far]
+
+    for copy in ca:
+        copy.wait_recv()
+    a2_own[...] = total(a_own, a_recv, z).astype(BF16)
     c2 = []
     for k in (4, 3, 5, 2, 6, 1, 7):
         c2.append(push(a2_own.at[turn(y, k)], a2_recv.at[k], a2_s.at[k], a2_r.at[k], at_y(k)))
-    b2_own[...] = ring_end(b_own, b_recv, y, cb).astype(BF16)
+    for copy in cb:
+        copy.wait_recv()
+    b2_own[...] = total(b_own, b_recv, y).astype(BF16)
     for k in (4, 3, 5, 2, 6, 1, 7):
         c2.append(push(b2_own.at[turn(z, k)], b2_recv.at[k], b2_s.at[k], b2_r.at[k], at_z(k)))
 
     for copy in ct:
         copy.wait_recv()
-
-    def total(own, recv, base):
-        acc = own[base].astype(F32)
-        for k in range(1, 8):
-            acc += recv[k].astype(F32)
-        return acc
 
     t3_own[...] = total(t1_own, t1_recv, z).astype(BF16)
     t4_own[...] = total(t2_own, t2_recv, y).astype(BF16)
@@ -299,6 +301,11 @@
     for k in (4, 3, 5, 2, 6, 1, 7):
         c3.append(push(t3_own.at[turn(y, k)], t3_recv.at[k], t3_s.at[k], t3_r.at[k], at_y(k)))
         c3.append(push(t4_own.at[turn(z, k)], t4_recv.at[k], t4_s.at[k], t4_r.at[k], at_z(k)))
+
+    for copy in co2:
+        copy.wait_recv()
+    o3_own[...] = total(o2_own, o2_recv, z).astype(BF16)
+    co3 = [push(o3_own, o3_recv.at[k], o3_s.at[k], o3_r.at[k], at_y(k)) for k in far]
 
     for copy in c2:
         copy.wait_recv()
@@ -313,8 +320,7 @@
                 if g != xl:
                     piece = pltpu.roll(piece, 32 * ((g - xl) % 4), 1)
                 acc = jnp.where(quarter == g, piece, acc)
-            both = jnp.concatenate([acc, a_cell[32 + 8 * xh:40 + 8 * xh]], axis=0)
-            x_own[xh * 4 + xl] = both.astype(BF16)
+            x_own[xh * 4 + xl] = acc
     cx = []
     for k in (4, 3, 5, 2, 6, 1, 7):
         cx.append(push(x_own.at[turn(x, k)], x_recv.at[k], x_s.at[k], x_r.at[k], at_x(k)))
@@ -328,23 +334,37 @@
     touched_ref[:, 256:384] = right[0:8]
     touched_ref[:, 384:512] = right[8:16]
 
+    for copy in co3:
+        copy.wait_recv()
+    flip[...] = o3_own[...].astype(F32)
+    for k in range(1, 8):
+        flip[...] += o3_recv[k].astype(F32)
+    part = flip[pl.ds(pl.multiple_of(lax.rem(y, 2) * 8, 8), 8), :]
+    acc = part
+    for g in range(1, 4):
+        acc = jnp.where(lax.div(y, 2) == g, pltpu.roll(part, 128 - 32 * g, 1), acc)
+    last_ref[8:16, :] = acc
     for copy in cx:
         copy.wait_recv()
+    last_ref[0:8, :] = total(x_own, x_recv, x)
+
+    for copy in sent:
+        copy.wait_send()
+
+
+def finish(rows_ref, last_ref, touched_ref, gin_ref, gout_ref):
+    touched_ref[...] = rows_ref[...]
     scale = 1.0 / math.sqrt(TOK * 16 * 64)
-    last = total(x_own, x_recv, x) * scale
-    turned = jnp.transpose(jnp.concatenate([last, jnp.zeros((112, 128), F32)], axis=0))
-    flip[...] = turned
+    tall = jnp.concatenate([last_ref[...] * scale, jnp.zeros((112, 128), F32)], axis=0)
+    turned = jnp.transpose(tall)
     for g in range(4):
         gin_ref[:, 8 * g:8 * g + 8] = turned[32 * g:32 * g + 32, 0:8]
-    gout_ref[...] = flip[pl.ds(pl.multiple_of(lax.rem(x, 4) * 32, 32), 32), :][:, 8:16]
-
-    for copy in sent:
-        copy.wait_send()
+    gout_ref[...] = last_ref[8:16, 0:32] * scale
 
 
 def on_device(tokens, cotangent, hist_len, item_owner, item_slot, w_in, w_out):
     vmem = pl.BlockSpec(memory_space=pltpu.VMEM)
-    hbm = pl.BlockSpec(memory_space=pl.ANY)
+    hbm = pl.BlockSpec(memory_space=pltpu.HBM)
 
     def buf(*shape, dtype=BF16):
         return pltpu.VMEM(shape, dtype)
@@ -352,35 +372,49 @@
     def sems(n):
         return pltpu.SemaphoreType.DMA((n,))
 
-    return pl.pallas_call(
+    rows, last = pl.pallas_call(
         kernel,
         out_shape=(
             jax.ShapeDtypeStruct((8, 512), F32),
-            jax.ShapeDtypeStruct((32, 32), F32),
-            jax.ShapeDtypeStruct((32, 8), F32),
+            jax.ShapeDtypeStruct((16, 128), F32),
         ),
-        in_specs=[pl.BlockSpec(memory_space=pltpu.SMEM), vmem, vmem, vmem, vmem, hbm, hbm],
-        out_specs=(vmem, vmem, vmem),
+        in_specs=[hbm] * 7,
+        out_specs=(vmem, vmem),
         scratch_shapes=[
+            pltpu.SMEM((2,), jnp.int32), buf(TOK, D), buf(TOK, D),
+            buf(1, TOK, dtype=jnp.int32), buf(1, TOK, dtype=jnp.int32),
             buf(512, 2048), buf(512, 512), buf(TOK, 2048, dtype=F32), buf(TOK, 2048),
             buf(256, 2048), buf(256, 256), buf(256, 256), buf(256, 512),
             buf(2, TOK, 256), buf(2, TOK, 256),
             buf(16, 16, 640), buf(16, 16, 640),
-            buf(8, 8, 48, 128), buf(7, 8, 48, 128), buf(8, 8, 32, 128), buf(7, 8, 32, 128),
+            buf(8, 8, 32, 128), buf(8, 8, 32, 128), buf(8, 8, 32, 128), buf(8, 8, 32, 128),
             buf(8, 8, 16, 128), buf(8, 8, 16, 128), buf(8, 8, 16, 128), buf(8, 8, 16, 128),
-            buf(8, 48, 128), buf(8, 48, 128), buf(8, 32, 128), buf(8, 32, 128),
+            buf(8, 32, 128), buf(8, 32, 128), buf(8, 32, 128), buf(8, 32, 128),
             buf(8, 16, 128), buf(8, 16, 128), buf(8, 16, 128), buf(8, 16, 128),
-            buf(8, 16, 128), buf(8, 16, 128), buf(128, 128, dtype=F32),
-            sems(5), sems(7), sems(7), sems(16), sems(16),
-            sems(7), sems(7), sems(7), sems(7),
-        ] + [sems(8)] * 14,
+            buf(8, 8, 128, dtype=F32), buf(8, 8, 128, dtype=F32),
+            buf(8, 32, 512), buf(8, 32, 512), buf(8, 16, 128), buf(8, 16, 128),
+            buf(16, 128), buf(8, 16, 128), buf(16, 128, dtype=F32),
+            sems(10), sems(7), sems(7), sems(16), sems(16),
+        ] + [sems(8)] * 24,
         compiler_params=pltpu.CompilerParams(
-            collective_id=0, has_side_effects=True, vmem_limit_bytes=40 * 1024 * 1024
+            collective_id=0, has_side_effects=True, vmem_limit_bytes=62 * 1024 * 1024
         ),
     )(
         hist_len, tokens, cotangent, item_owner.reshape(1, TOK), item_slot.reshape(1, TOK),
         w_in, w_out,
     )
+    touched, grad_in, grad_out = pl.pallas_call(
+        finish,
+        out_shape=(
+            jax.ShapeDtypeStruct((8, 512), F32),
+            jax.ShapeDtypeStruct((32, 32), F32),
+            jax.ShapeDtypeStruct((8, 32), F32),
+        ),
+        in_specs=[vmem, vmem],
+        out_specs=(vmem, vmem, vmem),
+        compiler_params=pltpu.CompilerParams(vmem_limit_bytes=62 * 1024 * 1024),
+    )(rows, last)
+    return touched, grad_in, grad_out.T
 
 
 def solution(mesh):

time: 69.6 us -> 58.9 us (0.85)
  local copies, waits for them, and re-layouts: 8.27 us -> 0 us
  Pallas kernels: 59.8 us -> 58 us
    unnamed x16 -> x0, local copies, waits for them, and re-layouts: 7.61 us -> none
    pallas_call x1, Pallas kernels: 59.8 us -> 56.5 us  [on_device(): pl.pallas_call(kernel, out_shape=(jax.ShapeDtypeStruct((8, 512), F32), ja...]
    pallas_call x0 -> x1, Pallas kernels: none -> 1.5 us  [on_device(): pl.pallas_call(finish, out_shape=(jax.ShapeDtypeStruct((8, 512), F32), ja...]
where the time goes in v2:
time: 58.9 us; the launch traced here: 58.7 us
  Pallas kernels  58 us (98%)
  between operations  0.64 us (1%)
    pallas_call x1, Pallas kernels, on_device(): pl.pallas_call(kernel, out_shape=(jax.ShapeDtypeStruct((8, 512), F32), ja...  56.5 us
    pallas_call x1, Pallas kernels, on_device(): pl.pallas_call(finish, out_shape=(jax.ShapeDtypeStruct((8, 512), F32), ja...  1.5 us

profile of v2, /device:TPU:1, one launch (start us, length us, event | category | flops | bytes accessed | tf_op | source)
XLA Modules:
  0.0 58.7 jit_solution(7012331175806067233)
XLA Ops:
  0.6 56.5 %shard_map.94 = (f32[8,512]{1,0:T(8,128)}, f32[16,128]{1,0:T(8,128)}) custom-call(s32[2]{0:T(128)} %len_hbm.1, bf16[128,512]{1,0:T(8,128)(2,1)} %tok_hbm.1, bf16[128,512]{1,0:T(8,128)(2,1)} %cot_hbm.1, s32[1,128]{1,0:T(1,128)} %bitcast.3, s32[1,128]{1,0:T(1,128)} %bitcast.4, bf16[512,2048]{1,0:T(8,128)(2,1)} %w_in_hbm.1, bf16[512,512]{1,0:T(8,128)(2,1)} %w_out_hbm.1), custom_call_target="tpu_custom_call" | custom-call | tf_op jit(solution)/shard_map/pallas_call | solution.py:375
  57.2 1.5 %shard_map.95 = (f32[8,512]{1,0:T(8,128)}, f32[32,32]{1,0:T(8,128)}, f32[8,32]{1,0:T(8,128)}) custom-call(f32[8,512]{1,0:T(8,128)} %get-tuple-element.8.rows_ref, f32[16,128]{1,0:T(8,128)} %get-tuple-element.9.last_ref), custom_call_target="tpu_custom_call" | custom-call | tf_op jit(solution)/shard_map/pallas_call | solution.py:406

commit v3 on v2

--- a/solution.py
+++ b/solution.py
@@ -54,13 +54,13 @@
     len_hbm, tok_hbm, cot_hbm, own_hbm, slot_hbm, w_in_hbm, w_out_hbm,
     touched_ref, last_ref,
     len_ref, tok_ref, cot_ref, own_ref, slot_ref, w_in, w_out, sgrad, hid, d2, nb2, gt2, er2, nbf, gtf,
-    out_rows, in_rows, a_own, a_recv, b_own, b_recv,
+    out_rows, in_rows, out_nums, in_nums, a_own, a_recv, a_late, b_own, b_recv, b_late,
     t1_own, t1_recv, t2_own, t2_recv,
     a2_own, a2_recv, b2_own, b2_recv, t3_own, t3_recv, t4_own, t4_recv,
     x_own, x_recv, o1_own, o1_recv, o2_own, o2_recv, o3_own, o3_recv, flip,
     w_sem, pair_s, pair_r, row_s, row_r, a_s, a_r, b_s, b_r,
     t1_s, t1_r, t2_s, t2_r, a2_s, a2_r, b2_s, b2_r, t3_s, t3_r, t4_s, t4_r, x_s, x_r,
-    o1_s, o1_r, o2_s, o2_r, o3_s, o3_r,
+    o1_s, o1_r, o2_s, o2_r, o3_s, o3_r, al_s, al_r, bl_s, bl_r, num_s, num_r,
 ):
     t = lax.axis_index("table")
     r = lax.axis_index("rep")
@@ -86,19 +86,20 @@
     sent = []
 
     def push(src, dst, ssem, rsem, where):
-        copy = pltpu.make_async_remote_copy(
+        pltpu.make_async_remote_copy(
             src_ref=src, dst_ref=dst, send_sem=ssem, recv_sem=rsem,
             device_id=where, device_id_type=MESH,
-        )
-        copy.start()
-        sent.append(copy)
-        return copy
-
-    barrier = pltpu.get_barrier_semaphore()
-    partners = [at_z(k) for k in range(1, 8)] + [at_y(k) for k in range(1, 8)]
-    partners += [at_t(k) for k in range(1, 16)]
-    for where in partners:
-        pl.semaphore_signal(barrier, inc=1, device_id=where, device_id_type=MESH)
+        ).start()
+
+    def settle(ref, sem):
+        pltpu.make_async_copy(ref, ref, sem).wait()
+
+    far = (4, 3, 5, 2, 6, 1, 7)
+
+    def spread(own, recv, ssem, rsem, base, where):
+        for k in far:
+            push(own.at[turn(base, k)], recv.at[k], ssem, rsem, where(k))
+        sent.append((own.at[pl.ds(0, 7)], ssem))
 
     small = []
     for n, (there, here) in enumerate((
@@ -113,6 +114,12 @@
     loads.append(pltpu.make_async_copy(w_out_hbm, w_out, w_sem.at[4]))
     for load in loads:
         load.start()
+
+    barrier = pltpu.get_barrier_semaphore()
+    partners = [at_z(k) for k in range(1, 8)] + [at_y(k) for k in range(1, 8)]
+    partners += [at_t(k) for k in range(1, 16)]
+    for where in partners:
+        pl.semaphore_signal(barrier, inc=1, device_id=where, device_id_type=MESH)
 
     small[1].wait()
     len0, len1 = len_ref[0], len_ref[1]
@@ -144,10 +151,9 @@
         hid[:, cols] = (pre * sig).astype(BF16)
         sgrad[:, cols] = sig * (1.0 + pre * (1.0 - sig))
     pl.semaphore_wait(barrier, len(partners))
-    pair = [
-        push(er2.at[pl.ds(0, TOK)], er2.at[pl.ds(TOK, TOK)], pair_s.at[0], pair_r.at[0], mate),
-        push(nbf.at[1 - core], nb2.at[pl.ds(TOK, TOK)], pair_s.at[1], pair_r.at[1], mate),
-    ]
+    own_half, mate_half = pl.ds(0, TOK), pl.ds(TOK, TOK)
+    push(er2.at[own_half], er2.at[mate_half], pair_s.at[0], pair_r.at[0], mate)
+    push(nbf.at[1 - core], nb2.at[mate_half], pair_s.at[1], pair_r.at[1], mate)
     score_scale = 1.0 / math.sqrt(DH)
     atts, slopes, mixes = [], [], []
     for h in range(HEADS):
@@ -167,7 +173,7 @@
     gtf[0] = gtp[:, :256]
     gtf[1] = gtp[:, 256:]
     gt2[0:TOK, :] = gtf[core]
-    pair.append(push(gtf.at[1 - core], gt2.at[pl.ds(TOK, TOK)], pair_s.at[2], pair_r.at[2], mate))
+    push(gtf.at[1 - core], gt2.at[mate_half], pair_s.at[2], pair_r.at[2], mate)
 
     loads[4].wait()
     dgate = mm(err, w_out[...], NT)
@@ -175,10 +181,7 @@
     def give(b, value):
         cols = pl.ds(b * 512, 512)
         d2[0:TOK, cols] = (value * sgrad[:, cols]).astype(BF16)
-        pair.append(push(
-            d2.at[pl.ds(0, TOK), cols], d2.at[pl.ds(TOK, TOK), cols],
-            pair_s.at[3 + b], pair_r.at[3 + b], mate,
-        ))
+        push(d2.at[own_half, cols], d2.at[mate_half, cols], pair_s.at[3], pair_r.at[3], mate)
 
     give(0, dgate * on_mix)
     dmix = norm_back(dgate * gate, on_mix, inv_mix).astype(BF16)
@@ -204,35 +207,33 @@
     small[4].wait()
     owner = own_ref[...]
     slot = slot_ref[...]
-    mine = iota((16, TOK), 0) == owner
-    hot = jnp.where(mine, 1.0, 0.0)
+    ahead = lax.rem(owner - t + 16, 16)
+    hot = jnp.where(iota((16, TOK), 0) == ahead, 1.0, 0.0)
     before = jnp.where(ri < ci, 1.0, 0.0).astype(BF16)
     earlier = mm(hot.astype(BF16), before)
     placed = jnp.sum(earlier * hot, axis=0, keepdims=True)
-    key = owner.astype(F32) * 16.0 + placed
+    key = ahead.astype(F32) * 16.0 + placed
     pick = jnp.where(iota((256, TOK), 0).astype(F32) == key, 1.0, 0.0)
-    packed = mm(pick.astype(BF16), rows).astype(BF16)
-    s_z = jnp.sum(pick * (slot // 64).astype(F32), axis=1, keepdims=True)
-    s_y = jnp.sum(pick * ((slot // 8) % 8).astype(F32), axis=1, keepdims=True)
-    s_i = jnp.sum(pick * (slot % 8).astype(F32), axis=1, keepdims=True)
-    lane = iota((256, 128), 1)
-    tail = jnp.where(lane == 0, s_z, jnp.where(lane == 1, s_y, jnp.where(lane == 2, s_i, 0.0)))
-    out_rows[:, :, 0:512] = packed.reshape(16, 16, 512)
-    out_rows[:, :, 512:640] = tail.astype(BF16).reshape(16, 16, 128)
-    in_rows[0] = out_rows[t]
-    row_copies = []
+    out_rows[...] = mm(pick.astype(BF16), rows).astype(BF16).reshape(16, 16, 512)
+    line = lax.rem(ahead, 8).astype(F32) * 16.0 + placed
+    spot = jnp.where(ri.astype(F32) == line, 1.0, 0.0).astype(BF16)
+    high = mm((hot * (slot // 16).astype(F32)).astype(BF16), spot, NT)
+    low = mm((hot * (slot % 16).astype(F32)).astype(BF16), spot, NT)
+    numbers = high * 16.0 + low
+    for k in range(16):
+        out_nums[k] = numbers[k:k + 1, :]
     for k in (8, 7, 9, 6, 10, 5, 11, 4, 12, 3, 13, 2, 14, 1, 15):
-        row_copies.append(push(
-            out_rows.at[turn(t, k, 16)], in_rows.at[k], row_s.at[k], row_r.at[k], at_t(k)
-        ))
-
-    for copy in pair[:3]:
-        copy.wait_recv()
+        push(out_nums.at[k], in_nums.at[k], num_s, num_r, at_t(k))
+        push(out_rows.at[k], in_rows.at[k], row_s, row_r, at_t(k))
+    in_rows[0] = out_rows[0]
+    in_nums[0] = out_nums[0]
+
+    settle(er2.at[mate_half], pair_r.at[0])
+    settle(nb2.at[mate_half], pair_r.at[1])
+    settle(gt2.at[mate_half], pair_r.at[2])
     o1_own[...] = mm(gt2[...], er2[...], TN).astype(BF16).reshape(8, 32, 512)
-    far = (4, 3, 5, 2, 6, 1, 7)
-    co1 = [push(o1_own.at[turn(x, k)], o1_recv.at[k], o1_s.at[k], o1_r.at[k], at_x(k)) for k in far]
-    for copy in pair[3:]:
-        copy.wait_recv()
+    spread(o1_own, o1_recv, o1_s, o1_r, x, at_x)
+    settle(d2.at[mate_half], pair_r.at[3])
 
     def block(k):
         d = turn(z, k)
@@ -241,76 +242,90 @@
         a_own[d] = part[:, :128].reshape(8, 32, 128).astype(BF16)
         b_own[:, d] = part[:, 128:].reshape(8, 32, 128).astype(BF16)
 
-    def spread(own, recv, ssem, rsem, base, where, k):
-        return push(own.at[turn(base, k)], recv.at[k], ssem.at[k], rsem.at[k], where(k))
-
-    ca, cb = [], []
-    for k in far:
+    for k in (4, 3, -3, 2, -2, 1, -1, 0):
         block(k)
-        ca.append(spread(a_own, a_recv, a_s, a_r, z, at_z, k))
-    block(0)
-    for k in far:
-        cb.append(spread(b_own, b_recv, b_s, b_r, y, at_y, k))
-
-    def total(own, recv, base):
+
+    def sides(base):
+        side = 1 - 2 * lax.rem(base, 2)
+        return ((pl.ds(0, 4), side), (pl.ds(4, 4), -side))
+
+    def swap(own, recv, ssem, rsem, base, where):
+        for j in (3, 2, 1, 0):
+            for part, side in sides(base):
+                push(
+                    own.at[turn(base, side * (j + 1)), part], recv.at[j, part],
+                    ssem, rsem, where(side),
+                )
+        sent.append((own.at[pl.ds(0, 4)], ssem))
+
+    def send_on(own, recv, got, late, ssem, rsem, base, where):
+        settle(recv, got)
+        for j in (3, 2, 1, 0):
+            for part, side in sides(base):
+                d = turn(base, -side * j)
+                own[d, part] = (own[d, part].astype(F32) + recv[j, part].astype(F32)).astype(BF16)
+                if j > 0:
+                    push(
+                        own.at[d, part], late.at[j - 1, part], ssem, rsem, where(-side * j)
+                    )
+        sent.append((own.at[pl.ds(0, 3)], ssem))
+
+    def gather(own, late, rsem, base):
+        settle(late, rsem)
+        acc = own[base].astype(F32)
+        for j in range(3):
+            acc += late[j].astype(F32)
+        return acc
+
+    swap(a_own, a_recv, a_s, a_r, z, at_z)
+    swap(b_own, b_recv, b_s, b_r, y, at_y)
+    send_on(a_own, a_recv, a_r, a_late, al_s, al_r, z, at_z)
+    send_on(b_own, b_recv, b_r, b_late, bl_s, bl_r, y, at_y)
+
+    def total(own, recv, rsem, base):
+        settle(recv.at[pl.ds(1, 7)], rsem)
         acc = own[base].astype(F32)
         for k in range(1, 8):
             acc += recv[k].astype(F32)
         return acc
 
-    for copy in row_copies:
-        copy.wait_recv()
-    arrived = in_rows[...].reshape(256, 640)
-    numbers = arrived[:, 512:640].astype(F32)
-    by_z = jnp.where(lane == 0, 64.0, jnp.where(lane == 1, 8.0, jnp.where(lane == 2, 1.0, 0.0)))
-    by_y = jnp.where(lane == 0, 8.0, jnp.where(lane == 1, 64.0, jnp.where(lane == 2, 1.0, 0.0)))
-    line = iota((256, 512), 1).astype(F32)
-    hot_z = jnp.where(line == jnp.sum(numbers * by_z, axis=1, keepdims=True), 1.0, 0.0)
-    hot_y = jnp.where(line == jnp.sum(numbers * by_y, axis=1, keepdims=True), 1.0, 0.0)
-    t1_own[...] = cells(mm(hot_z.astype(BF16), arrived[:, 0:256], TN))
-    t2_own[...] = cells(mm(hot_y.astype(BF16), arrived[:, 256:512], TN))
-    ct = []
-    for k in (4, 3, 5, 2, 6, 1, 7):
-        ct.append(push(t1_own.at[turn(z, k)], t1_recv.at[k], t1_s.at[k], t1_r.at[k], at_z(k)))
-        ct.append(push(t2_own.at[turn(y, k)], t2_recv.at[k], t2_s.at[k], t2_r.at[k], at_y(k)))
-
-    for copy in co1:
-        copy.wait_recv()
-    tall = jnp.transpose(total(o1_own, o1_recv, x)).reshape(8, 4, 16, 32)
+    settle(in_nums.at[pl.ds(1, 15)], num_r)
+    settle(in_rows.at[pl.ds(1, 15)], row_r)
+    arrived = in_rows[...].reshape(256, 512)
+    first, second = in_nums[0], in_nums[8]
+    for k in range(1, 8):
+        first += in_nums[k]
+        second += in_nums[8 + k]
+    named = jnp.concatenate([first, second], axis=1).astype(jnp.int32)
+    place = iota((512, 256), 0)
+    hot_z = jnp.where(place == named, 1.0, 0.0).astype(BF16)
+    place = (place // 8 % 8) * 64 + (place // 64) * 8 + place % 8
+    hot_y = jnp.where(place == named, 1.0, 0.0).astype(BF16)
+    t1_own[...] = cells(mm(hot_z, arrived[:, 0:256]))
+    t2_own[...] = cells(mm(hot_y, arrived[:, 256:512]))
+    spread(t1_own, t1_recv, t1_s, t1_r, z, at_z)
+    spread(t2_own, t2_recv, t2_s, t2_r, y, at_y)
+
+    tall = jnp.transpose(total(o1_own, o1_recv, o1_r, x)).reshape(8, 4, 16, 32)
     o2_own[...] = jnp.concatenate([tall[:, g] for g in range(4)], axis=-1).astype(BF16)
-    co2 = [push(o2_own.at[turn(z, k)], o2_recv.at[k], o2_s.at[k], o2_r.at[k], at_z(k)) for k in far]
-
-    for copy in ca:
-        copy.wait_recv()
-    a2_own[...] = total(a_own, a_recv, z).astype(BF16)
-    c2 = []
-    for k in (4, 3, 5, 2, 6, 1, 7):
-        c2.append(push(a2_own.at[turn(y, k)], a2_recv.at[k], a2_s.at[k], a2_r.at[k], at_y(k)))
-    for copy in cb:
-        copy.wait_recv()
-    b2_own[...] = total(b_own, b_recv, y).astype(BF16)
-    for k in (4, 3, 5, 2, 6, 1, 7):
-        c2.append(push(b2_own.at[turn(z, k)], b2_recv.at[k], b2_s.at[k], b2_r.at[k], at_z(k)))
-
-    for copy in ct:
-        copy.wait_recv()
-
-    t3_own[...] = total(t1_own, t1_recv, z).astype(BF16)
-    t4_own[...] = total(t2_own, t2_recv, y).astype(BF16)
-    c3 = []
-    for k in (4, 3, 5, 2, 6, 1, 7):
-        c3.append(push(t3_own.at[turn(y, k)], t3_recv.at[k], t3_s.at[k], t3_r.at[k], at_y(k)))
-        c3.append(push(t4_own.at[turn(z, k)], t4_recv.at[k], t4_s.at[k], t4_r.at[k], at_z(k)))
-
-    for copy in co2:
-        copy.wait_recv()
-    o3_own[...] = total(o2_own, o2_recv, z).astype(BF16)
-    co3 = [push(o3_own, o3_recv.at[k], o3_s.at[k], o3_r.at[k], at_y(k)) for k in far]
-
-    for copy in c2:
-        copy.wait_recv()
-    a_cell = total(a2_own, a2_recv, y)
-    b_cell = total(b2_own, b2_recv, z)
+    spread(o2_own, o2_recv, o2_s, o2_r, z, at_z)
+    a2_own[...] = gather(a_own, a_late, al_r, z).astype(BF16)
+    spread(a2_own, a2_recv, a2_s, a2_r, y, at_y)
+    b2_own[...] = gather(b_own, b_late, bl_r, y).astype(BF16)
+    spread(b2_own, b2_recv, b2_s, b2_r, z, at_z)
+
+    t3_own[...] = total(t1_own, t1_recv, t1_r, z).astype(BF16)
+    spread(t3_own, t3_recv, t3_s, t3_r, y, at_y)
+    t4_own[...] = total(t2_own, t2_recv, t2_r, y).astype(BF16)
+    spread(t4_own, t4_recv, t4_s, t4_r, z, at_z)
+
+    o3_own[...] = total(o2_own, o2_recv, o2_r, z).astype(BF16)
+    for k in far:
+        push(o3_own, o3_recv.at[k], o3_s, o3_r, at_y(k))
+    sent.append((o3_recv.at[pl.ds(0, 7)], o3_s))
+
+    a_cell = total(a2_own, a2_recv, a2_r, y)
+    b_cell = total(b2_own, b2_recv, b2_r, z)
     quarter = iota((8, 128), 1) // 32
     for xh, source_cell in ((0, a_cell), (1, b_cell)):
         for xl in range(4):
@@ -321,21 +336,16 @@
                     piece = pltpu.roll(piece, 32 * ((g - xl) % 4), 1)
                 acc = jnp.where(quarter == g, piece, acc)
             x_own[xh * 4 + xl] = acc
-    cx = []
-    for k in (4, 3, 5, 2, 6, 1, 7):
-        cx.append(push(x_own.at[turn(x, k)], x_recv.at[k], x_s.at[k], x_r.at[k], at_x(k)))
-
-    for copy in c3:
-        copy.wait_recv()
-    left = total(t3_own, t3_recv, y)
-    right = total(t4_own, t4_recv, z)
+    spread(x_own, x_recv, x_s, x_r, x, at_x)
+
+    left = total(t3_own, t3_recv, t3_r, y)
+    right = total(t4_own, t4_recv, t4_r, z)
     touched_ref[:, 0:128] = left[0:8]
     touched_ref[:, 128:256] = left[8:16]
     touched_ref[:, 256:384] = right[0:8]
     touched_ref[:, 384:512] = right[8:16]
 
-    for copy in co3:
-        copy.wait_recv()
+    settle(o3_recv.at[pl.ds(1, 7)], o3_r)
     flip[...] = o3_own[...].astype(F32)
     for k in range(1, 8):
         flip[...] += o3_recv[k].astype(F32)
@@ -344,12 +354,16 @@
     for g in range(1, 4):
         acc = jnp.where(lax.div(y, 2) == g, pltpu.roll(part, 128 - 32 * g, 1), acc)
     last_ref[8:16, :] = acc
-    for copy in cx:
-        copy.wait_recv()
-    last_ref[0:8, :] = total(x_own, x_recv, x)
-
-    for copy in sent:
-        copy.wait_send()
+    last_ref[0:8, :] = total(x_own, x_recv, x_r, x)
+
+    sent.append((er2.at[own_half], pair_s.at[0]))
+    sent.append((nbf.at[0], pair_s.at[1]))
+    sent.append((gtf.at[0], pair_s.at[2]))
+    sent.append((d2.at[own_half], pair_s.at[3]))
+    sent.append((out_rows.at[pl.ds(1, 15)], row_s))
+    sent.append((out_nums.at[pl.ds(1, 15)], num_s))
+    for ref, sem in sent:
+        settle(ref, sem)
 
 
 def finish(rows_ref, last_ref, touched_ref, gin_ref, gout_ref):
@@ -386,16 +400,18 @@
             buf(512, 2048), buf(512, 512), buf(TOK, 2048, dtype=F32), buf(TOK, 2048),
             buf(256, 2048), buf(256, 256), buf(256, 256), buf(256, 512),
             buf(2, TOK, 256), buf(2, TOK, 256),
-            buf(16, 16, 640), buf(16, 16, 640),
-            buf(8, 8, 32, 128), buf(8, 8, 32, 128), buf(8, 8, 32, 128), buf(8, 8, 32, 128),
+            buf(16, 16, 512), buf(16, 16, 512),
+            buf(16, 1, 128, dtype=F32), buf(16, 1, 128, dtype=F32),
+            buf(8, 8, 32, 128), buf(4, 8, 32, 128), buf(3, 8, 32, 128),
+            buf(8, 8, 32, 128), buf(4, 8, 32, 128), buf(3, 8, 32, 128),
             buf(8, 8, 16, 128), buf(8, 8, 16, 128), buf(8, 8, 16, 128), buf(8, 8, 16, 128),
             buf(8, 32, 128), buf(8, 32, 128), buf(8, 32, 128), buf(8, 32, 128),
             buf(8, 16, 128), buf(8, 16, 128), buf(8, 16, 128), buf(8, 16, 128),
             buf(8, 8, 128, dtype=F32), buf(8, 8, 128, dtype=F32),
             buf(8, 32, 512), buf(8, 32, 512), buf(8, 16, 128), buf(8, 16, 128),
             buf(16, 128), buf(8, 16, 128), buf(16, 128, dtype=F32),
-            sems(10), sems(7), sems(7), sems(16), sems(16),
-        ] + [sems(8)] * 24,
+            sems(10), sems(4), sems(4),
+        ] + [pltpu.SemaphoreType.DMA] * 32,
         compiler_params=pltpu.CompilerParams(
             collective_id=0, has_side_effects=True, vmem_limit_bytes=62 * 1024 * 1024
         ),

time: 58.9 us -> 54 us (0.917)
  Pallas kernels: 58 us -> 53 us
    pallas_call x1, Pallas kernels: 56.5 us -> 51.5 us  [on_device(): pl.pallas_call(kernel, out_shape=(jax.ShapeDtypeStruct((8, 512), F32), ja...]
where the time goes in v3:
time: 54 us; the launch traced here: 53.6 us
  Pallas kernels  53 us (98%)
  between operations  0.64 us (1%)
    pallas_call x1, Pallas kernels, on_device(): pl.pallas_call(kernel, out_shape=(jax.ShapeDtypeStruct((8, 512), F32), ja...  51.5 us
    pallas_call x1, Pallas kernels, on_device(): pl.pallas_call(finish, out_shape=(jax.ShapeDtypeStruct((8, 512), F32), ja...  1.5 us

profile of v3, /device:TPU:1, one launch (start us, length us, event | category | flops | bytes accessed | tf_op | source)
XLA Modules:
  0.0 53.6 jit_solution(11023471615110083166)
XLA Ops:
  0.6 51.5 %shard_map.94 = (f32[8,512]{1,0:T(8,128)}, f32[16,128]{1,0:T(8,128)}) custom-call(s32[2]{0:T(128)} %len_hbm.1, bf16[128,512]{1,0:T(8,128)(2,1)} %tok_hbm.1, bf16[128,512]{1,0:T(8,128)(2,1)} %cot_hbm.1, s32[1,128]{1,0:T(1,128)} %bitcast.3, s32[1,128]{1,0:T(1,128)} %bitcast.4, bf16[512,2048]{1,0:T(8,128)(2,1)} %w_in_hbm.1, bf16[512,512]{1,0:T(8,128)(2,1)} %w_out_hbm.1), custom_call_target="tpu_custom_call" | custom-call | tf_op jit(solution)/shard_map/pallas_call | solution.py:389
  52.1 1.5 %shard_map.95 = (f32[8,512]{1,0:T(8,128)}, f32[32,32]{1,0:T(8,128)}, f32[8,32]{1,0:T(8,128)}) custom-call(f32[8,512]{1,0:T(8,128)} %get-tuple-element.8.rows_ref, f32[16,128]{1,0:T(8,128)} %get-tuple-element.9.last_ref), custom_call_target="tpu_custom_call" | custom-call | tf_op jit(solution)/shard_map/pallas_call | solution.py:422

commit v4 on v3

--- a/solution.py
+++ b/solution.py
@@ -55,12 +55,13 @@
     touched_ref, last_ref,
     len_ref, tok_ref, cot_ref, own_ref, slot_ref, w_in, w_out, sgrad, hid, d2, nb2, gt2, er2, nbf, gtf,
     out_rows, in_rows, out_nums, in_nums, a_own, a_recv, a_late, b_own, b_recv, b_late,
-    t1_own, t1_recv, t2_own, t2_recv,
+    t1_own, t1_recv, t1_late, t2_own, t2_recv, t2_late,
     a2_own, a2_recv, b2_own, b2_recv, t3_own, t3_recv, t4_own, t4_recv,
     x_own, x_recv, o1_own, o1_recv, o2_own, o2_recv, o3_own, o3_recv, flip,
     w_sem, pair_s, pair_r, row_s, row_r, a_s, a_r, b_s, b_r,
     t1_s, t1_r, t2_s, t2_r, a2_s, a2_r, b2_s, b2_r, t3_s, t3_r, t4_s, t4_r, x_s, x_r,
     o1_s, o1_r, o2_s, o2_r, o3_s, o3_r, al_s, al_r, bl_s, bl_r, num_s, num_r,
+    tl1_s, tl1_r, tl2_s, tl2_r,
 ):
     t = lax.axis_index("table")
     r = lax.axis_index("rep")
@@ -143,6 +144,25 @@
     small[2].wait()
     err = jnp.where(valid, cot_ref[...], jnp.zeros((TOK, D), BF16))
     er2[0:TOK, :] = err
+    small[3].wait()
+    small[4].wait()
+    owner = own_ref[...]
+    slot = slot_ref[...]
+    ahead = lax.rem(owner - t + 16, 16)
+    hot = jnp.where(iota((16, TOK), 0) == ahead, 1.0, 0.0)
+    before = jnp.where(ri < ci, 1.0, 0.0).astype(BF16)
+    earlier = mm(hot.astype(BF16), before)
+    placed = jnp.sum(earlier * hot, axis=0, keepdims=True)
+    key = ahead.astype(F32) * 16.0 + placed
+    pick = jnp.where(iota((256, TOK), 0).astype(F32) == key, 1.0, 0.0)
+    pick = pick.astype(BF16)
+    line = lax.rem(ahead, 8).astype(F32) * 16.0 + placed
+    spot = jnp.where(ri.astype(F32) == line, 1.0, 0.0).astype(BF16)
+    high = mm((hot * (slot // 16).astype(F32)).astype(BF16), spot, NT)
+    low = mm((hot * (slot % 16).astype(F32)).astype(BF16), spot, NT)
+    numbers = high * 16.0 + low
+    for k in range(16):
+        out_nums[k] = numbers[k:k + 1, :]
     for b in range(4):
         cols = pl.ds(b * 512, 512)
         loads[b].wait()
@@ -203,25 +223,7 @@
         dnorm += mm(d2[0:TOK, b * 512:(b + 1) * 512], w_in[:, b * 512:(b + 1) * 512], NT)
     rows = (err.astype(F32) + norm_back(dnorm, normed, inv_tok)).astype(BF16)
 
-    small[3].wait()
-    small[4].wait()
-    owner = own_ref[...]
-    slot = slot_ref[...]
-    ahead = lax.rem(owner - t + 16, 16)
-    hot = jnp.where(iota((16, TOK), 0) == ahead, 1.0, 0.0)
-    before = jnp.where(ri < ci, 1.0, 0.0).astype(BF16)
-    earlier = mm(hot.astype(BF16), before)
-    placed = jnp.sum(earlier * hot, axis=0, keepdims=True)
-    key = ahead.astype(F32) * 16.0 + placed
-    pick = jnp.where(iota((256, TOK), 0).astype(F32) == key, 1.0, 0.0)
-    out_rows[...] = mm(pick.astype(BF16), rows).astype(BF16).reshape(16, 16, 512)
-    line = lax.rem(ahead, 8).astype(F32) * 16.0 + placed
-    spot = jnp.where(ri.astype(F32) == line, 1.0, 0.0).astype(BF16)
-    high = mm((hot * (slot // 16).astype(F32)).astype(BF16), spot, NT)
-    low = mm((hot * (slot % 16).astype(F32)).astype(BF16), spot, NT)
-    numbers = high * 16.0 + low
-    for k in range(16):
-        out_nums[k] = numbers[k:k + 1, :]
+    out_rows[...] = mm(pick, rows).astype(BF16).reshape(16, 16, 512)
     for k in (8, 7, 9, 6, 10, 5, 11, 4, 12, 3, 13, 2, 14, 1, 15):
         push(out_nums.at[k], in_nums.at[k], num_s, num_r, at_t(k))
         push(out_rows.at[k], in_rows.at[k], row_s, row_r, at_t(k))
@@ -303,26 +305,19 @@
     hot_y = jnp.where(place == named, 1.0, 0.0).astype(BF16)
     t1_own[...] = cells(mm(hot_z, arrived[:, 0:256]))
     t2_own[...] = cells(mm(hot_y, arrived[:, 256:512]))
-    spread(t1_own, t1_recv, t1_s, t1_r, z, at_z)
-    spread(t2_own, t2_recv, t2_s, t2_r, y, at_y)
-
-    tall = jnp.transpose(total(o1_own, o1_recv, o1_r, x)).reshape(8, 4, 16, 32)
-    o2_own[...] = jnp.concatenate([tall[:, g] for g in range(4)], axis=-1).astype(BF16)
-    spread(o2_own, o2_recv, o2_s, o2_r, z, at_z)
+    swap(t1_own, t1_recv, t1_s, t1_r, z, at_z)
+    swap(t2_own, t2_recv, t2_s, t2_r, y, at_y)
+
     a2_own[...] = gather(a_own, a_late, al_r, z).astype(BF16)
     spread(a2_own, a2_recv, a2_s, a2_r, y, at_y)
     b2_own[...] = gather(b_own, b_late, bl_r, y).astype(BF16)
     spread(b2_own, b2_recv, b2_s, b2_r, z, at_z)
-
-    t3_own[...] = total(t1_own, t1_recv, t1_r, z).astype(BF16)
-    spread(t3_own, t3_recv, t3_s, t3_r, y, at_y)
-    t4_own[...] = total(t2_own, t2_recv, t2_r, y).astype(BF16)
-    spread(t4_own, t4_recv, t4_s, t4_r, z, at_z)
-
-    o3_own[...] = total(o2_own, o2_recv, o2_r, z).astype(BF16)
-    for k in far:
-        push(o3_own, o3_recv.at[k], o3_s, o3_r, at_y(k))
-    sent.append((o3_recv.at[pl.ds(0, 7)], o3_s))
+    send_on(t1_own, t1_recv, t1_r, t1_late, tl1_s, tl1_r, z, at_z)
+    send_on(t2_own, t2_recv, t2_r, t2_late, tl2_s, tl2_r, y, at_y)
+
+    tall = jnp.transpose(total(o1_own, o1_recv, o1_r, x)).reshape(8, 4, 16, 32)
+    o2_own[...] = jnp.concatenate([tall[:, g] for g in range(4)], axis=-1).astype(BF16)
+    spread(o2_own, o2_recv, o2_s, o2_r, z, at_z)
 
     a_cell = total(a2_own, a2_recv, a2_r, y)
     b_cell = total(b2_own, b2_recv, b2_r, z)
@@ -338,6 +333,17 @@
             x_own[xh * 4 + xl] = acc
     spread(x_own, x_recv, x_s, x_r, x, at_x)
 
+    t3_own[...] = gather(t1_own, t1_late, tl1_r, z).astype(BF16)
+    spread(t3_own, t3_recv, t3_s, t3_r, y, at_y)
+    t4_own[...] = gather(t2_own, t2_late, tl2_r, y).astype(BF16)
+    spread(t4_own, t4_recv, t4_s, t4_r, z, at_z)
+
+    o3_own[...] = total(o2_own, o2_recv, o2_r, z).astype(BF16)
+    for k in far:
+        push(o3_own, o3_recv.at[k], o3_s, o3_r, at_y(k))
+    sent.append((o3_recv.at[pl.ds(0, 7)], o3_s))
+
+    last_ref[0:8, :] = total(x_own, x_recv, x_r, x)
     left = total(t3_own, t3_recv, t3_r, y)
     right = total(t4_own, t4_recv, t4_r, z)
     touched_ref[:, 0:128] = left[0:8]
@@ -354,7 +360,6 @@
     for g in range(1, 4):
         acc = jnp.where(lax.div(y, 2) == g, pltpu.roll(part, 128 - 32 * g, 1), acc)
     last_ref[8:16, :] = acc
-    last_ref[0:8, :] = total(x_own, x_recv, x_r, x)
 
     sent.append((er2.at[own_half], pair_s.at[0]))
     sent.append((nbf.at[0], pair_s.at[1]))
@@ -404,14 +409,15 @@
             buf(16, 1, 128, dtype=F32), buf(16, 1, 128, dtype=F32),
             buf(8, 8, 32, 128), buf(4, 8, 32, 128), buf(3, 8, 32, 128),
             buf(8, 8, 32, 128), buf(4, 8, 32, 128), buf(3, 8, 32, 128),
-            buf(8, 8, 16, 128), buf(8, 8, 16, 128), buf(8, 8, 16, 128), buf(8, 8, 16, 128),
+            buf(8, 8, 16, 128), buf(4, 8, 16, 128), buf(3, 8, 16, 128),
+            buf(8, 8, 16, 128), buf(4, 8, 16, 128), buf(3, 8, 16, 128),
             buf(8, 32, 128), buf(8, 32, 128), buf(8, 32, 128), buf(8, 32, 128),
             buf(8, 16, 128), buf(8, 16, 128), buf(8, 16, 128), buf(8, 16, 128),
             buf(8, 8, 128, dtype=F32), buf(8, 8, 128, dtype=F32),
             buf(8, 32, 512), buf(8, 32, 512), buf(8, 16, 128), buf(8, 16, 128),
             buf(16, 128), buf(8, 16, 128), buf(16, 128, dtype=F32),
             sems(10), sems(4), sems(4),
-        ] + [pltpu.SemaphoreType.DMA] * 32,
+        ] + [pltpu.SemaphoreType.DMA] * 36,
         compiler_params=pltpu.CompilerParams(
             collective_id=0, has_side_effects=True, vmem_limit_bytes=62 * 1024 * 1024
         ),

time: 54 us -> 53.3 us (0.987)
  Pallas kernels: 53 us -> 51.9 us
    pallas_call x1, Pallas kernels: 51.5 us -> 50.4 us  [on_device(): pl.pallas_call(kernel, out_shape=(jax.ShapeDtypeStruct((8, 512), F32), ja...]
where the time goes in v4:
time: 53.3 us; the launch traced here: 52.5 us
  Pallas kernels  51.9 us (97%)
  between operations  0.64 us (1%)
    pallas_call x1, Pallas kernels, on_device(): pl.pallas_call(kernel, out_shape=(jax.ShapeDtypeStruct((8, 512), F32), ja...  50.4 us
    pallas_call x1, Pallas kernels, on_device(): pl.pallas_call(finish, out_shape=(jax.ShapeDtypeStruct((8, 512), F32), ja...  1.5 us

profile of v4, /device:TPU:1, one launch (start us, length us, event | category | flops | bytes accessed | tf_op | source)
XLA Modules:
  0.0 52.5 jit_solution(7616342605186182406)
XLA Ops:
  0.6 50.4 %shard_map.94 = (f32[8,512]{1,0:T(8,128)}, f32[16,128]{1,0:T(8,128)}) custom-call(s32[2]{0:T(128)} %len_hbm.1, bf16[128,512]{1,0:T(8,128)(2,1)} %tok_hbm.1, bf16[128,512]{1,0:T(8,128)(2,1)} %cot_hbm.1, s32[1,128]{1,0:T(1,128)} %bitcast.3, s32[1,128]{1,0:T(1,128)} %bitcast.4, bf16[512,2048]{1,0:T(8,128)(2,1)} %w_in_hbm.1, bf16[512,512]{1,0:T(8,128)(2,1)} %w_out_hbm.1), custom_call_target="tpu_custom_call" | custom-call | tf_op jit(solution)/shard_map/pallas_call | solution.py:394
  51.0 1.5 %shard_map.95 = (f32[8,512]{1,0:T(8,128)}, f32[32,32]{1,0:T(8,128)}, f32[8,32]{1,0:T(8,128)}) custom-call(f32[8,512]{1,0:T(8,128)} %get-tuple-element.8.rows_ref, f32[16,128]{1,0:T(8,128)} %get-tuple-element.9.last_ref), custom_call_target="tpu_custom_call" | custom-call | tf_op jit(solution)/shard_map/pallas_call | solution.py:428

commit v5 on v4

--- a/solution.py
+++ b/solution.py
@@ -244,20 +244,20 @@
         a_own[d] = part[:, :128].reshape(8, 32, 128).astype(BF16)
         b_own[:, d] = part[:, 128:].reshape(8, 32, 128).astype(BF16)
 
-    for k in (4, 3, -3, 2, -2, 1, -1, 0):
-        block(k)
-
     def sides(base):
         side = 1 - 2 * lax.rem(base, 2)
         return ((pl.ds(0, 4), side), (pl.ds(4, 4), -side))
 
+    def swap_step(own, recv, ssem, rsem, base, where, j):
+        for part, side in sides(base):
+            push(
+                own.at[turn(base, side * (j + 1)), part], recv.at[j, part],
+                ssem, rsem, where(side),
+            )
+
     def swap(own, recv, ssem, rsem, base, where):
         for j in (3, 2, 1, 0):
-            for part, side in sides(base):
-                push(
-                    own.at[turn(base, side * (j + 1)), part], recv.at[j, part],
-                    ssem, rsem, where(side),
-                )
+            swap_step(own, recv, ssem, rsem, base, where, j)
         sent.append((own.at[pl.ds(0, 4)], ssem))
 
     def send_on(own, recv, got, late, ssem, rsem, base, where):
@@ -279,7 +279,12 @@
             acc += late[j].astype(F32)
         return acc
 
-    swap(a_own, a_recv, a_s, a_r, z, at_z)
+    for j, made in ((3, (4,)), (2, (3, -3)), (1, (2, -2)), (0, (1, -1))):
+        for k in made:
+            block(k)
+        swap_step(a_own, a_recv, a_s, a_r, z, at_z, j)
+    sent.append((a_own.at[pl.ds(0, 4)], a_s))
+    block(0)
     swap(b_own, b_recv, b_s, b_r, y, at_y)
     send_on(a_own, a_recv, a_r, a_late, al_s, al_r, z, at_z)
     send_on(b_own, b_recv, b_r, b_late, bl_s, bl_r, y, at_y)
@@ -301,11 +306,11 @@
     named = jnp.concatenate([first, second], axis=1).astype(jnp.int32)
     place = iota((512, 256), 0)
     hot_z = jnp.where(place == named, 1.0, 0.0).astype(BF16)
+    t1_own[...] = cells(mm(hot_z, arrived[:, 0:256]))
+    swap(t1_own, t1_recv, t1_s, t1_r, z, at_z)
     place = (place // 8 % 8) * 64 + (place // 64) * 8 + place % 8
     hot_y = jnp.where(place == named, 1.0, 0.0).astype(BF16)
-    t1_own[...] = cells(mm(hot_z, arrived[:, 0:256]))
     t2_own[...] = cells(mm(hot_y, arrived[:, 256:512]))
-    swap(t1_own, t1_recv, t1_s, t1_r, z, at_z)
     swap(t2_own, t2_recv, t2_s, t2_r, y, at_y)
 
     a2_own[...] = gather(a_own, a_late, al_r, z).astype(BF16)

time: 53.3 us -> 52.9 us (level); the launches traced: 52.5 us -> 52.7 us
  no operation moved by 1% of the time
where the time goes in v5:
time: 52.9 us; the launch traced here: 52.7 us
  Pallas kernels  52 us (98%)
  between operations  0.64 us (1%)
    pallas_call x1, Pallas kernels, on_device(): pl.pallas_call(kernel, out_shape=(jax.ShapeDtypeStruct((8, 512), F32), ja...  50.5 us
    pallas_call x1, Pallas kernels, on_device(): pl.pallas_call(finish, out_shape=(jax.ShapeDtypeStruct((8, 512), F32), ja...  1.5 us

profile of v5, /device:TPU:1, one launch (start us, length us, event | category | flops | bytes accessed | tf_op | source)
XLA Modules:
  0.0 52.7 jit_solution(6735867052759803726)
XLA Ops:
  0.6 50.5 %shard_map.94 = (f32[8,512]{1,0:T(8,128)}, f32[16,128]{1,0:T(8,128)}) custom-call(s32[2]{0:T(128)} %len_hbm.1, bf16[128,512]{1,0:T(8,128)(2,1)} %tok_hbm.1, bf16[128,512]{1,0:T(8,128)(2,1)} %cot_hbm.1, s32[1,128]{1,0:T(1,128)} %bitcast.3, s32[1,128]{1,0:T(1,128)} %bitcast.4, bf16[512,2048]{1,0:T(8,128)(2,1)} %w_in_hbm.1, bf16[512,512]{1,0:T(8,128)(2,1)} %w_out_hbm.1), custom_call_target="tpu_custom_call" | custom-call | tf_op jit(solution)/shard_map/pallas_call | solution.py:399
  51.2 1.5 %shard_map.95 = (f32[8,512]{1,0:T(8,128)}, f32[32,32]{1,0:T(8,128)}, f32[8,32]{1,0:T(8,128)}) custom-call(f32[8,512]{1,0:T(8,128)} %get-tuple-element.8.rows_ref, f32[16,128]{1,0:T(8,128)} %get-tuple-element.9.last_ref), custom_call_target="tpu_custom_call" | custom-call | tf_op jit(solution)/shard_map/pallas_call | solution.py:433
